TPU v7x, 512 devices: a whole 4x4x16 slice. The times are simulated.
512 devices in a mesh: row: 32 (over y, x, core), col: 16 (over z).
Axes of the slice: x: 4, y: 4, z: 16, core: 2. Of those that a mesh axis runs over, the one named last changes fastest.
Arguments:
- blocks: float32 [16, 96, 4, 256, 256], P('col', 'row'), may hold values from -0.046875 to 0.046875
- block_cols: int32 [16, 96, 4], P('col', 'row'), may hold values from 0 to 191, as said below
- block_slot: int32 [16, 192], P('col'), may hold values from 0 to 191, as said below
- trials: float32 [16, 192, 32, 256], P('col', 'row'), may hold values from -6 to 6
- basis: float32 [32, 24576], P(None, ('row', 'col'))
- ritz_terms: float32 [32, 32], replicated, may hold values from -332.55374 to 332.55374
Outputs:
- sigma: float32 [32, 24576], P(None, ('row', 'col'))
- corrections: float32 [32, 24576], P(None, ('row', 'col'))
Inputs may be any that keep to these rules, and one draw needn't show every extreme that they name: `block_slot`: each row of one column group is a permutation of the storage slots 0 to 191. `block_cols`: the 12 block columns of one device (its 3 block rows) are all different; among them at most 1 have storage slots on one index of row (slot // 6 equal), and some index has exactly 1.
All inputs are finite; a program needn't handle non-finite values.
Results may differ from a plain program's by a relative error of at most 0.00014.
Values sent between devices are 32-bit elements; how exact they have to be, the bound alone decides.
No kernel may reach another device: no remote copies, remote signals or barrier semaphores. Data moves between devices by JAX's collectives and lax.ppermute only.
A program may use at most 64 MiB of HBM per device.

v0:
```python
import jax
import jax.numpy as jnp
from jax import lax
from jax.sharding import PartitionSpec as P


def per_device(blocks, block_cols, block_slot, trials, basis, ritz_terms):
    high = lax.Precision.HIGHEST
    local_blocks = blocks[0]
    rows_here = local_blocks.shape[0]
    per_row = local_blocks.shape[1]
    size = local_blocks.shape[2]
    count = rows_here * per_row
    stored = trials[0]
    vectors = stored.shape[1]
    table = block_slot[0]
    columns = block_cols[0].reshape(count)
    positions = jnp.arange(table.shape[0], dtype=jnp.int32)
    slots = jnp.sum(jnp.where(columns[:, None] == positions[None, :], table[None, :], 0), axis=1)
    gathered = lax.all_gather(stored, "row", axis=0, tiled=True)
    chosen = gathered[slots]
    chosen = chosen.reshape(rows_here, per_row, vectors, size)
    partial_value = jnp.einsum("rnij,rnkj->kri", local_blocks, chosen, precision=high)
    partial_value = partial_value.reshape(vectors, rows_here * size)
    sigma = lax.psum_scatter(partial_value, "col", scatter_dimension=1, tiled=True)
    resid = sigma - jnp.dot(ritz_terms.T, basis, precision=high)
    first = lax.psum(jnp.dot(basis, resid.T, precision=high), ("row", "col"))
    projected = resid - jnp.dot(first.T, basis, precision=high)
    second = lax.psum(jnp.dot(basis, projected.T, precision=high), ("row", "col"))
    corrections = projected - jnp.dot(second.T, basis, precision=high)
    return (sigma, corrections)


def solution(mesh):
    in_specs = (
        P("col", "row", None, None, None),
        P("col", "row", None),
        P("col", None),
        P("col", "row", None, None),
        P(None, ("row", "col")),
        P(),
    )
    out_specs = (P(None, ("row", "col")), P(None, ("row", "col")))
    return jax.shard_map(
        per_device, mesh=mesh, in_specs=in_specs, out_specs=out_specs, check_vma=False
    )
```

profile of v0, /device:TPU:1, one launch (start us, length us, event | category | flops | bytes accessed | tf_op | source)
XLA Modules:
  0.0 369.2 jit_solution(4045464523241503938)
XLA Ops:
  7.2 0.0 copy-start
  7.2 0.0 copy-start.1
  7.2 0.0 all-gather.3.cloned.1.call-start
  7.2 0.7 all-gather.3.cloned.1.call-update
  7.9 0.0 reduce-scatter.4.cloned.1.call-start
  8.0 0.9 reduce
  8.8 0.1 eq.15
  8.9 0.9 select_reduce_fusion
  9.8 0.6 pad_clamp_fusion
  10.4 71.0 %all-gather.3.cloned.1.call-done = f32[1,192,32,256]{3,2,0,1:T(8,128)} async-done(((f32[1,6,32,256]{3,2,0,1:T(8,128)}), f32[1,192,32,256]{3,2,0,1:T(8,128)}) %all-gather.3.cloned.1.call-update) | async-done | bytes 6291472 | tf_op jit(solution)/shard_map/all_gather | solution.py:20
  81.3 3.5 gather_fusion
  84.8 0.0 copy-done
  84.8 3.6 fusion.2
  88.4 1.8 copy.16
  90.2 0.0 reduce-scatter.4.cloned.1.call-update
  90.2 56.8 %reduce-scatter.4.cloned.1.call-done = f32[48,32]{1,0:T(8,128)} async-done(((f32[768,32]{1,0:T(8,128)}), f32[48,32]{1,0:T(8,128)}) %reduce-scatter.4.cloned.1.call-update) | async-done | bytes 6160
  147.1 0.8 copy.15
  147.9 0.0 copy-done.1
  147.9 0.0 copy-start.2
  147.9 0.9 convolution_subtract_fusion.2
  148.8 0.1 convolution_bitcast_fusion.1
  149.0 112.2 %psum.14 = f32[32,32]{0,1:T(8,128)S(1)} all-reduce(f32[32,32]{0,1:T(8,128)S(1)} %convolution_bitcast_fusion.1), channel_id=1, replica_groups=mesh['row'=32,'col'=16] {'row','col'}, use_global_device_ids=true, to_apply=%region_2.3 | all-reduce | flops 1024 | bytes 8192 | tf_op jit(solution)/shard_map/psum | solution.py:27
  261.1 0.1 convolution_subtract_fusion.1
  261.3 0.2 convolution_bitcast_fusion
  261.4 100.2 %psum.15 = f32[32,32]{0,1:T(8,128)S(1)} all-reduce(f32[32,32]{0,1:T(8,128)S(1)} %convolution_bitcast_fusion), channel_id=1, replica_groups=mesh['row'=32,'col'=16] {'row','col'}, use_global_device_ids=true, to_apply=%region_3.4 | all-reduce | flops 1024 | bytes 8192 | tf_op jit(solution)/shard_map/psum | solution.py:29
  361.6 0.7 convolution_subtract_fusion
  362.3 0.0 copy-done.2
  (1 shorter events, 0.0 us)
Async XLA Ops:
  7.2 77.7 %copy-start = (f32[1,3,4,256,256]{4,3,2,1,0:T(8,128)S(1)}, f32[1,3,4,256,256]{4,3,2,1,0:T(8,128)}, u32[]{:S(2)}) copy-start(f32[1,3,4,256,256]{4,3,2,1,0:T(8,128)} %param.6) | copy-start | bytes 9437188
  7.2 140.7 %copy-start.1 = (f32[32,48]{1,0:T(8,128)S(1)}, f32[32,48]{1,0:T(8,128)}, u32[]{:S(2)}) copy-start(f32[32,48]{1,0:T(8,128)} %param.10) | copy-start | bytes 18436
  7.2 74.2 %all-gather.3.cloned.1.call-start = ((), (), s32[]{:S(2)}) async-start(), calls=%async_computation.1 | async-start | bytes 6488064 | tf_op jit(solution)/shard_map/all_gather | solution.py:20
  7.9 139.1 %reduce-scatter.4.cloned.1.call-start = ((), (), s32[]{:S(2)}) async-start(), calls=%async_computation.2 | async-start | bytes 417792
  147.9 214.5 %copy-start.2 = (f32[32,48]{1,0:T(8,128)}, f32[32,48]{1,0:T(8,128)S(1)}, u32[]{:S(2)}) copy-start(f32[32,48]{1,0:T(8,128)S(1)} %copy.15) | copy-start | bytes 18436
Sparse Core Ops, SparseCore 0:
  11.2 70.1 all-gather.2
  90.3 56.6 reduce-scatter.3
where the time goes:
time: 370 us; the launch traced here: 369 us
  blocking collectives  212 us (57%)
  waiting for transfers between devices  128 us (35%)
  between operations  14.1 us (4%)
  local copies, waits for them, and re-layouts  6.18 us (2%)
  matrix products  5.67 us (2%)
    psum x1, blocking collectives, per_device(): first = lax.psum(jnp.dot(basis, resid.T, precision=high), ('row', 'col'))  112 us
    psum x1, blocking collectives, per_device(): lax.psum(jnp.dot(basis, projected.T, precision=high), ('row', 'col'))  100 us
    all_gather x1, waiting for transfers between devices, per_device(): gathered = lax.all_gather(stored, 'row', axis=0, tiled=True)  71 us
    unnamed x3, waiting for transfers between devices  57.5 us
  transfers between devices with their start and end apart: 2, of which 2 were waited for; matrix products, arithmetic and copies ran while one was open for 1% of the time, Pallas kernels for 0%

commit v1 on v0

v1 whole, which is shorter than its diff:
```python
import functools

import jax
import jax.numpy as jnp
from jax import lax
from jax.experimental import pallas as pl
from jax.experimental.pallas import tpu as pltpu
from jax.sharding import PartitionSpec as P

LANES = 128
HIGH = lax.Precision.HIGHEST
SMEM = pl.BlockSpec(memory_space=pltpu.SMEM)
VMEM = pl.BlockSpec(memory_space=pltpu.VMEM)
NT = (((1,), (1,)), ((), ()))
TN = (((0,), (0,)), ((), ()))


def slot_of(cols_ref, table_ref, entry):
    return table_ref[cols_ref[entry]]


def request_kernel(stored, cols_ref, table_ref, out_ref):
    owners = lax.broadcasted_iota(jnp.int32, out_ref.shape, 0)
    wanted = jnp.zeros(out_ref.shape, jnp.int32)
    for entry in range(cols_ref.shape[0]):
        slot = slot_of(cols_ref, table_ref, entry)
        owner = slot // stored
        wanted = jnp.where(owners == owner, slot - owner * stored, wanted)
    out_ref[...] = wanted


def pick_kernel(wanted_ref, trials_ref, out_ref):
    for dest in range(out_ref.shape[0]):
        out_ref[dest] = trials_ref[wanted_ref[dest, 0]]


def split(value):
    top = value.astype(jnp.bfloat16)
    rest = (value - top.astype(jnp.float32)).astype(jnp.bfloat16)
    return top, rest


def partial_kernel(
    stored, cols_ref, table_ref, blocks_ref, chosen_ref, basis_ref, out_ref, gram_ref, part, wide, bwide
):
    rows, per_row, size, _ = blocks_ref.shape
    vectors = chosen_ref.shape[1]
    groups, _, width = basis_ref.shape
    for row in range(rows):
        total = jnp.zeros((vectors, size), jnp.float32)
        for entry in range(per_row):
            owner = slot_of(cols_ref, table_ref, row * per_row + entry) // stored
            vec_top, vec_rest = split(chosen_ref[owner])
            mat_top, mat_rest = split(blocks_ref[row, entry])
            both = jnp.concatenate([vec_top, vec_rest], axis=0)
            first = lax.dot_general(both, mat_top, NT, preferred_element_type=jnp.float32)
            second = lax.dot_general(vec_top, mat_rest, NT, preferred_element_type=jnp.float32)
            total += first[:vectors] + (first[vectors:] + second)
        part[:, row * size : (row + 1) * size] = total
    chunk = rows * size // groups
    pad = jnp.zeros((vectors, LANES - chunk), jnp.float32)
    for group in range(groups):
        wide[:, group * LANES : (group + 1) * LANES] = jnp.concatenate(
            [part[:, group * chunk : (group + 1) * chunk], pad], axis=1
        )
        bwide[:, group * LANES : (group + 1) * LANES] = jnp.concatenate([basis_ref[group], pad], axis=1)
    moments = lax.dot_general(bwide[...], wide[...], NT, precision=HIGH, preferred_element_type=jnp.float32)
    gram_ref[...] = lax.dot_general(
        bwide[...], bwide[...], NT, precision=HIGH, preferred_element_type=jnp.float32
    )
    for group in range(groups):
        out_ref[group] = wide[:, group * LANES : (group + 1) * LANES]
        out_ref[group, :, chunk : chunk + vectors] = moments


def sum_kernel(recv_ref, gram_ref, sigma_ref, out_ref):
    groups = recv_ref.shape[0]
    chunk = sigma_ref.shape[1]
    nb = gram_ref.shape[0]
    total = recv_ref[0]
    for group in range(1, groups):
        total = total + recv_ref[group]
    sigma_ref[...] = total[:, :chunk]
    moments = total[:, chunk : chunk + nb]
    gram = gram_ref[...]
    half = nb // 2
    packed = jnp.concatenate([moments[:half], moments[half:], gram[:half], gram[half:]], axis=1)
    for dest in range(out_ref.shape[0]):
        out_ref[dest] = packed


def final_kernel(recv_ref, sigma_ref, basis_ref, ritz_ref, out_ref):
    total = recv_ref[0]
    for source in range(1, recv_ref.shape[0]):
        total = total + recv_ref[source]
    nb = ritz_ref.shape[0]
    moments = jnp.concatenate([total[:, :nb], total[:, nb : 2 * nb]], axis=0)
    gram = jnp.concatenate([total[:, 2 * nb : 3 * nb], total[:, 3 * nb :]], axis=0)
    ritz = ritz_ref[...]
    dot = functools.partial(jnp.dot, precision=HIGH, preferred_element_type=jnp.float32)
    first = moments - dot(gram, ritz)
    second = first - dot(gram, first)
    weights = ritz + first + second
    out_ref[...] = sigma_ref[...] - lax.dot_general(
        weights, basis_ref[...], TN, precision=HIGH, preferred_element_type=jnp.float32
    )


def shape(*dims, dtype=jnp.float32):
    return jax.ShapeDtypeStruct(dims, dtype)


def per_device(n_row, n_col, blocks, block_cols, block_slot, trials, basis, ritz_terms):
    local = blocks[0]
    rows, per_row, size, _ = local.shape
    owned = trials[0]
    stored, vectors, _ = owned.shape
    nb, chunk = basis.shape
    cols = block_cols.reshape(rows * per_row)
    table = block_slot.reshape(block_slot.shape[1])
    params = pltpu.CompilerParams(vmem_limit_bytes=32 * 1024 * 1024)

    requests = pl.pallas_call(
        functools.partial(request_kernel, stored),
        out_shape=shape(n_row, LANES, dtype=jnp.int32),
        in_specs=[SMEM, SMEM],
        out_specs=VMEM,
        compiler_params=params,
    )(cols, table)
    wanted = lax.all_to_all(requests, "row", 0, 0, tiled=True)
    sent = pl.pallas_call(
        pick_kernel,
        out_shape=shape(n_row, vectors, size),
        in_specs=[SMEM, VMEM],
        out_specs=VMEM,
        compiler_params=params,
    )(wanted, owned)
    chosen = lax.all_to_all(sent, "row", 0, 0, tiled=True)
    spread = jnp.broadcast_to(basis[None], (n_col, nb, chunk))
    row_basis = lax.all_to_all(spread, "col", 0, 0, tiled=True)

    partial_sums, gram = pl.pallas_call(
        functools.partial(partial_kernel, stored),
        out_shape=(shape(n_col, vectors, LANES), shape(nb, nb)),
        in_specs=[SMEM, SMEM, VMEM, VMEM, VMEM],
        out_specs=(VMEM, VMEM),
        scratch_shapes=[
            pltpu.VMEM((vectors, rows * size), jnp.float32),
            pltpu.VMEM((vectors, n_col * LANES), jnp.float32),
            pltpu.VMEM((nb, n_col * LANES), jnp.float32),
        ],
        compiler_params=params,
    )(cols, table, local, chosen, row_basis)
    gathered = lax.all_to_all(partial_sums, "col", 0, 0, tiled=True)
    sigma, moments = pl.pallas_call(
        sum_kernel,
        out_shape=(shape(vectors, chunk), shape(n_row, nb // 2, LANES)),
        in_specs=[VMEM, VMEM],
        out_specs=(VMEM, VMEM),
        compiler_params=params,
    )(gathered, gram)
    all_moments = lax.all_to_all(moments, "row", 0, 0, tiled=True)
    corrections = pl.pallas_call(
        final_kernel,
        out_shape=shape(vectors, chunk),
        in_specs=[VMEM, VMEM, VMEM, VMEM],
        out_specs=VMEM,
        compiler_params=params,
    )(all_moments, sigma, basis, ritz_terms)
    return sigma, corrections


def solution(mesh):
    in_specs = (
        P("col", "row", None, None, None),
        P("col", "row", None),
        P("col", None),
        P("col", "row", None, None),
        P(None, ("row", "col")),
        P(),
    )
    out_specs = (P(None, ("row", "col")), P(None, ("row", "col")))
    body = functools.partial(per_device, mesh.shape["row"], mesh.shape["col"])
    return jax.shard_map(body, mesh=mesh, in_specs=in_specs, out_specs=out_specs, check_vma=False)
```

time: 370 us -> 111 us (0.30)
  blocking collectives: 212 us -> 34.2 us
  waiting for transfers between devices: 128 us -> 30.1 us
  starting transfers between devices: 0.08 us -> 29.6 us
  between operations: 14.1 us -> 0.7 us
  Pallas kernels: 0 us -> 7.68 us
  matrix products: 5.67 us -> 0 us
    psum x2 -> x0, blocking collectives: 212 us -> none  [the longest x1 112 us: per_device(): first = lax.psum(jnp.dot(basis, resid.T, precision=high), ('row', 'col'))]
    all_gather x1 -> x0, waiting for transfers between devices: 71 us -> none  [per_device(): gathered = lax.all_gather(stored, 'row', axis=0, tiled=True)]
    unnamed x3 -> x0, waiting for transfers between devices: 57.5 us -> none
    all_to_all x0 -> x2, blocking collectives: none -> 34.2 us  [the longest x1 17.2 us: per_device(): all_moments = lax.all_to_all(moments, 'row', 0, 0, tiled=True)]
    all_to_all x0 -> x3, waiting for transfers between devices: none -> 30.1 us  [the longest x1 15.7 us: per_device(): chosen = lax.all_to_all(sent, 'row', 0, 0, tiled=True)]
    all_to_all x0 -> x3, starting transfers between devices: none -> 29.6 us  [the longest x1 13 us: per_device(): row_basis = lax.all_to_all(spread, 'col', 0, 0, tiled=True)]
    pallas_call x0 -> x5, Pallas kernels: none -> 7.68 us  [the longest x1 2.68 us: per_device(): pl.pallas_call(functools.partial(partial_kernel, stored), out_shape=(shap...]
    dot_general x6 -> x0, matrix products: 5.67 us -> none  [the longest x1 3.55 us: per_device(): jnp.einsum('rnij,rnkj->kri', local_blocks, chosen, precision=high)]
  transfers between devices with their start and end apart: 2 -> 3, of which waited for: 2 -> 3; matrix products, arithmetic and copies ran while one was open for 1% -> 3% of each run, Pallas kernels for 0% -> 2%
where the time goes in v1:
time: 111 us
  blocking collectives  34.2 us (31%)
  waiting for transfers between devices  30.1 us (27%)
  starting transfers between devices  29.6 us (27%)
  Pallas kernels  7.68 us (7%)
  local copies, waits for them, and re-layouts  6.58 us (6%)
  other arithmetic  1.61 us (1%)
    all_to_all x1, blocking collectives, per_device(): all_moments = lax.all_to_all(moments, 'row', 0, 0, tiled=True)  17.2 us
    all_to_all x1, blocking collectives, per_device(): gathered = lax.all_to_all(partial_sums, 'col', 0, 0, tiled=True)  17 us
    all_to_all x1, waiting for transfers between devices, per_device(): chosen = lax.all_to_all(sent, 'row', 0, 0, tiled=True)  15.7 us
    all_to_all x1, starting transfers between devices, per_device(): row_basis = lax.all_to_all(spread, 'col', 0, 0, tiled=True)  13 us
    all_to_all x1, starting transfers between devices, per_device(): wanted = lax.all_to_all(requests, 'row', 0, 0, tiled=True)  10.4 us
    all_to_all x1, waiting for transfers between devices, per_device(): row_basis = lax.all_to_all(spread, 'col', 0, 0, tiled=True)  9.09 us
    all_to_all x1, starting transfers between devices, per_device(): chosen = lax.all_to_all(sent, 'row', 0, 0, tiled=True)  6.24 us
    all_to_all x1, waiting for transfers between devices, per_device(): wanted = lax.all_to_all(requests, 'row', 0, 0, tiled=True)  5.34 us
  transfers between devices with their start and end apart: 3, of which 3 were waited for; matrix products, arithmetic and copies ran while one was open for 3% of the time, Pallas kernels for 2%

profile of v1, /device:TPU:1, one launch (start us, length us, event | category | flops | bytes accessed | tf_op | source)
XLA Modules:
  0.0 110.5 jit_solution(5687498547273352192)
XLA Ops:
  0.6 0.0 copy-start.6
  0.6 0.7 reduce
  1.3 0.1 reshape.13.cols_ref
  1.4 0.0 copy-start.5
  1.4 0.7 copy-done.5
  2.1 1.2 %shard_map.77 = s32[32,128]{1,0:T(8,128)} custom-call(s32[12]{0:T(128)S(1)} %reshape.13.cols_ref, s32[192]{0:T(256)S(1)} %bitcast.10), custom_call_target="tpu_custom_call" | custom-call | tf_op jit(solution)/shard_map/pallas_call | solution.py:123
  3.3 10.4 %all-to-all-start = ((s32[32,1,128]{2,1,0:T(1,128)}), s32[32,1,128]{2,1,0:T(1,128)S(1)}, u32[]{:S(2)}, u32[]{:S(2)}) async-start(s32[32,1,128]{2,1,0:T(1,128)} %bitcast.3), calls=%async_computation | async-start | bytes 32768 | tf_op jit(solution)/shard_map/all_to_all | solution.py:130
  13.7 0.7 broadcast_in_dim.2
  14.5 0.9 reshape.16
  15.3 5.3 %all-to-all-done = s32[32,1,128]{2,1,0:T(1,128)S(1)} async-done(((s32[32,1,128]{2,1,0:T(1,128)}), s32[32,1,128]{2,1,0:T(1,128)S(1)}, u32[]{:S(2)}, u32[]{:S(2)}) %all-to-all-start) | async-done | bytes 16416 | tf_op jit(solution)/shard_map/all_to_all | solution.py:130
  20.7 13.0 %all-to-all-start.2 = ((f32[16,1,1536]{2,1,0:T(1,128)}), f32[16,1,1536]{2,1,0:T(1,128)S(1)}, u32[]{:S(2)}, u32[]{:S(2)}) async-start(f32[16,1,1536]{2,1,0:T(1,128)} %reshape.16), calls=%async_computation.2 | async-start | bytes 196608 | tf_op jit(solution)/shard_map/all_to_all | solution.py:140
  33.7 0.0 copy-start.1
  33.7 0.9 copy-done.1
  34.7 1.8 %shard_map.78 = f32[32,32,256]{2,1,0:T(8,128)} custom-call(s32[32,128]{1,0:T(8,128)S(1)} %bitcast.9, f32[6,32,256]{2,1,0:T(8,128)S(1)} %bitcast.8), custom_call_target="tpu_custom_call" | custom-call | tf_op jit(solution)/shard_map/pallas_call | solution.py:131
  36.5 9.1 %all-to-all-done.2 = f32[16,1,1536]{2,1,0:T(1,128)S(1)} async-done(((f32[16,1,1536]{2,1,0:T(1,128)}), f32[16,1,1536]{2,1,0:T(1,128)S(1)}, u32[]{:S(2)}, u32[]{:S(2)}) %all-to-all-start.2) | async-done | bytes 98336 | tf_op jit(solution)/shard_map/all_to_all | solution.py:140
  45.6 6.2 %all-to-all-start.1 = ((f32[32,32,256]{2,1,0:T(8,128)}), f32[32,32,256]{2,1,0:T(8,128)S(1)}, u32[]{:S(2)}, u32[]{:S(2)}) async-start(f32[32,32,256]{2,1,0:T(8,128)} %shard_map.78), calls=%async_computation.1 | async-start | bytes 2097152 | tf_op jit(solution)/shard_map/all_to_all | solution.py:138
  51.8 0.5 broadcast.2
  52.3 0.0 copy-start.2
  52.3 0.9 reduce.1
  53.3 0.1 reshape.17.basis_ref
  53.4 15.7 %all-to-all-done.1.chosen_ref = f32[32,32,256]{2,1,0:T(8,128)S(1)} async-done(((f32[32,32,256]{2,1,0:T(8,128)}), f32[32,32,256]{2,1,0:T(8,128)S(1)}, u32[]{:S(2)}, u32[]{:S(2)}) %all-to-all-start.1) | async-done | bytes 1048608 | tf_op jit(solution)/shard_map/all_to_all | solution.py:138
  69.1 0.0 copy-done.6
  69.1 0.0 copy-start
  69.1 1.9 %copy-done = f32[1,3,4,256,256]{4,3,2,1,0:T(8,128)S(1)} copy-done((f32[1,3,4,256,256]{4,3,2,1,0:T(8,128)S(1)}, f32[1,3,4,256,256]{4,3,2,1,0:T(8,128)}, u32[]{:S(2)}) %copy-start) | copy-done | bytes 3145752
  71.0 2.7 %shard_map.79 = (f32[16,32,128]{2,1,0:T(8,128)S(1)}, f32[32,32]{1,0:T(8,128)S(1)}) custom-call(s32[12]{0:T(128)S(1)} %reshape.13.cols_ref, s32[192]{0:T(256)S(1)} %bitcast.11, f32[3,4,256,256]{3,2,1,0:T(8,128)S(1)} %bitcast.7, f32[32,32,256]{2,1,0:T(8,128)S(1)} %all-to-all-done.1.chosen_ref, f32[16,32,48]{2,1,0:T(8,128)S(1)} %reshape.17.basis_ref), custom_call_target="tpu_custom_call" | custom-call | tf_op jit(solution)/shard_map/pallas_call | solution.py:142
  73.7 17.0 %all_to_all.31.recv_ref = f32[16,32,128]{2,1,0:T(8,128)S(1)} all-to-all(f32[16,32,128]{2,1,0:T(8,128)S(1)} %get-tuple-element.6), channel_id=1, replica_groups=mesh['row'=32,'col'=16] {'col'}, dimensions={0} | all-to-all | bytes 524288 | tf_op jit(solution)/shard_map/all_to_all | solution.py:154
  90.7 0.6 shard_map.80
  91.3 17.2 %all_to_all.32.recv_ref = f32[32,16,128]{2,1,0:T(8,128)S(1)} all-to-all(f32[32,16,128]{2,1,0:T(8,128)S(1)} %get-tuple-element.9), channel_id=1, replica_groups=mesh['row'=32,'col'=16] {'row'}, dimensions={0} | all-to-all | bytes 524288 | tf_op jit(solution)/shard_map/all_to_all | solution.py:162
  108.5 0.0 copy-done.2
  108.5 0.0 copy-done.3
  108.5 0.7 copy-done.4
  109.2 1.3 %shard_map.81 = f32[32,48]{1,0:T(8,128)} custom-call(f32[32,16,128]{2,1,0:T(8,128)S(1)} %all_to_all.32.recv_ref, f32[32,48]{1,0:T(8,128)S(1)} %copy-done.4, f32[32,48]{1,0:T(8,128)S(1)} %copy-done.2, f32[32,32]{1,0:T(8,128)S(1)} %copy-done.3), custom_call_target="tpu_custom_call" | custom-call | tf_op jit(solution)/shard_map/pallas_call | solution.py:163
  (2 shorter events, 0.0 us)
Async XLA Ops:
  0.6 68.5 %copy-start.6 = (s32[1,192]{1,0:T(1,128)S(1)}, s32[1,192]{1,0:T(1,128)}, u32[]{:S(2)}) copy-start(s32[1,192]{1,0:T(1,128)} %param.8) | copy-start | bytes 2308
  1.4 0.7 copy-start.5
  3.3 17.3 %all-to-all-start = ((s32[32,1,128]{2,1,0:T(1,128)}), s32[32,1,128]{2,1,0:T(1,128)S(1)}, u32[]{:S(2)}, u32[]{:S(2)}) async-start(s32[32,1,128]{2,1,0:T(1,128)} %bitcast.3), calls=%async_computation | async-start | bytes 32768 | tf_op jit(solution)/shard_map/all_to_all | solution.py:130
  20.7 24.9 %all-to-all-start.2 = ((f32[16,1,1536]{2,1,0:T(1,128)}), f32[16,1,1536]{2,1,0:T(1,128)S(1)}, u32[]{:S(2)}, u32[]{:S(2)}) async-start(f32[16,1,1536]{2,1,0:T(1,128)} %reshape.16), calls=%async_computation.2 | async-start | bytes 196608 | tf_op jit(solution)/shard_map/all_to_all | solution.py:140
  33.7 0.9 copy-start.1
  45.6 23.5 %all-to-all-start.1 = ((f32[32,32,256]{2,1,0:T(8,128)}), f32[32,32,256]{2,1,0:T(8,128)S(1)}, u32[]{:S(2)}, u32[]{:S(2)}) async-start(f32[32,32,256]{2,1,0:T(8,128)} %shard_map.78), calls=%async_computation.1 | async-start | bytes 2097152 | tf_op jit(solution)/shard_map/all_to_all | solution.py:138
  52.3 56.2 %copy-start.2 = (f32[32,48]{1,0:T(8,128)S(1)}, f32[32,48]{1,0:T(8,128)}, u32[]{:S(2)}) copy-start(f32[32,48]{1,0:T(8,128)} %basis_ref.1) | copy-start | bytes 18436
  52.3 56.2 %copy-start.3 = (f32[32,32]{1,0:T(8,128)S(1)}, f32[32,32]{1,0:T(8,128)}, u32[]{:S(2)}) copy-start(f32[32,32]{1,0:T(8,128)} %ritz_ref.1) | copy-start | bytes 12292
  69.1 1.9 %copy-start = (f32[1,3,4,256,256]{4,3,2,1,0:T(8,128)S(1)}, f32[1,3,4,256,256]{4,3,2,1,0:T(8,128)}, u32[]{:S(2)}) copy-start(f32[1,3,4,256,256]{4,3,2,1,0:T(8,128)} %param.6) | copy-start | bytes 9437188
  108.5 0.7 copy-start.4

commit v2 on v1

v2 whole, which is shorter than its diff:
```python
import functools

import jax
import jax.numpy as jnp
from jax import lax
from jax.experimental import pallas as pl
from jax.experimental.pallas import tpu as pltpu
from jax.sharding import PartitionSpec as P

LANES = 128
HIGH = lax.Precision.HIGHEST
SMEM = pl.BlockSpec(memory_space=pltpu.SMEM)
VMEM = pl.BlockSpec(memory_space=pltpu.VMEM)
HBM = pl.BlockSpec(memory_space=pltpu.HBM)
NT = (((1,), (1,)), ((), ()))
TN = (((0,), (0,)), ((), ()))
STEPS = (1, 8, 4, 2)
REQUEST_ROWS = 2
EARLY = 2


def slot_of(cols_ref, table_ref, row, entry):
    return table_ref[0, cols_ref[row, 0, entry]]


def request_kernel(
    cols_hbm, table_hbm, basis_hbm, trials_hbm, out_ref, packed_ref, trials_ref, cols, table, basis_ref, sems
):
    copies = [
        pltpu.make_async_copy(source, target, sems.at[index])
        for index, (source, target) in enumerate(
            [(cols_hbm, cols), (table_hbm, table), (basis_hbm, basis_ref), (trials_hbm, trials_ref)]
        )
    ]
    for copy in copies:
        copy.start()
    stored = trials_ref.shape[0]
    copies[0].wait()
    copies[1].wait()
    owners = lax.broadcasted_iota(jnp.int32, out_ref.shape, 0) // REQUEST_ROWS
    wanted = jnp.zeros(out_ref.shape, jnp.int32)
    for row in range(cols.shape[0]):
        for entry in range(cols.shape[2]):
            slot = slot_of(cols, table, row, entry)
            owner = slot // stored
            wanted = jnp.where(owners == owner, slot - owner * stored, wanted)
    out_ref[...] = wanted
    copies[2].wait()
    basis = basis_ref[...]
    half, chunk = basis.shape[0] // 2, basis.shape[1]
    pad = jnp.zeros((half, LANES - 2 * chunk), jnp.float32)
    packed_ref[0] = jnp.concatenate([basis[:half], basis[half:], pad], axis=1)
    copies[3].wait()


def join_kernel(left_ref, right_ref, out_ref):
    count = left_ref.shape[0]
    out_ref[:count] = left_ref[...]
    out_ref[count:] = right_ref[...]


def pick_kernel(wanted_ref, trials_ref, out_ref):
    dests, vectors, size = out_ref.shape
    stored = trials_ref.shape[0]
    for dest in range(dests):
        want = jnp.broadcast_to(wanted_ref[dest * REQUEST_ROWS : dest * REQUEST_ROWS + 1, :], (8, LANES))
        masks = [want == index for index in range(1, stored)]
        for top in range(0, vectors, 8):
            for left in range(0, size, LANES):
                tile = trials_ref[0, top : top + 8, left : left + LANES]
                for index in range(1, stored):
                    other = trials_ref[index, top : top + 8, left : left + LANES]
                    tile = jnp.where(masks[index - 1], other, tile)
                out_ref[dest, top : top + 8, left : left + LANES] = tile


def split(value):
    top = value.astype(jnp.bfloat16)
    rest = (value - top.astype(jnp.float32)).astype(jnp.bfloat16)
    return top, rest


def load_kernel(blocks_hbm, out_ref, sem):
    copy = pltpu.make_async_copy(blocks_hbm.at[: out_ref.shape[0]], out_ref, sem)
    copy.start()
    copy.wait()


def place_of(relative):
    place = 0
    for order, step in enumerate(STEPS):
        place = place + ((relative // step) % 2) * (1 << order)
    return place


def basis_kernel(packed_ref, out_ref):
    groups, half, _ = packed_ref.shape
    chunk = out_ref.shape[1] // groups
    own = lax.axis_index("col")
    for group in range(groups):
        both = packed_ref[place_of(jnp.bitwise_xor(own, group))]
        here = slice(group * chunk, (group + 1) * chunk)
        out_ref[:, here] = jnp.concatenate([both[:, :chunk], both[:, chunk : 2 * chunk]], axis=0)


def gram_kernel(basis_ref, out_ref):
    basis = basis_ref[...]
    out_ref[...] = lax.dot_general(basis, basis, NT, precision=HIGH, preferred_element_type=jnp.float32)


def partial_kernel(
    stored, cols_ref, table_ref, held_ref, blocks_hbm, chosen_ref, basis_ref, out_ref, part, late, sems
):
    rows, per_row, size, _ = blocks_hbm.shape
    held = held_ref.shape[0]
    vectors = chosen_ref.shape[1]
    groups = out_ref.shape[0]
    copies = [
        pltpu.make_async_copy(blocks_hbm.at[row], late.at[row - held], sems.at[row - held])
        for row in range(held, rows)
    ]
    for copy in copies:
        copy.start()
    for row in range(rows):
        if row >= held:
            copies[row - held].wait()
        total = jnp.zeros((vectors, size), jnp.float32)
        for entry in range(per_row):
            owner = slot_of(cols_ref, table_ref, row, entry) // stored
            vec_top, vec_rest = split(chosen_ref[owner])
            block = held_ref[row, entry] if row < held else late[row - held, entry]
            mat_top, mat_rest = split(block)
            both = jnp.concatenate([vec_top, vec_rest], axis=0)
            first = lax.dot_general(both, mat_top, NT, preferred_element_type=jnp.float32)
            second = lax.dot_general(vec_top, mat_rest, NT, preferred_element_type=jnp.float32)
            total += first[:vectors] + (first[vectors:] + second)
        part[:, row * size : (row + 1) * size] = total
    moments = lax.dot_general(
        basis_ref[...], part[...], NT, precision=HIGH, preferred_element_type=jnp.float32
    )
    half, quarter = vectors // 2, vectors // 4
    chunk = rows * size // groups
    pad = jnp.zeros((quarter, LANES - 2 * vectors), jnp.float32)
    low = jnp.concatenate([moments[half : half + quarter], moments[half + quarter :], pad], axis=1)
    for group in range(groups):
        here = slice(group * chunk, (group + 1) * chunk)
        out_ref[group, :half] = jnp.concatenate([part[:half, here], part[half:, here], moments[:half]], axis=1)
        out_ref[group, half:] = low


def sum_kernel(recv_ref, gram_ref, sigma_ref, keep_ref, out_ref):
    vectors, chunk = sigma_ref.shape
    half, quarter = vectors // 2, vectors // 4
    total = recv_ref[0]
    for group in range(1, recv_ref.shape[0]):
        total = total + recv_ref[group]
    sigma = jnp.concatenate([total[:half, :chunk], total[:half, chunk : 2 * chunk]], axis=0)
    sigma_ref[...] = sigma
    keep_ref[...] = sigma
    low = jnp.concatenate([total[half:, :vectors], total[half:, vectors : 2 * vectors]], axis=0)
    gram = gram_ref[...]
    packed = jnp.concatenate([total[:half, 2 * chunk :], low, gram[:half], gram[half:]], axis=1)
    for dest in range(out_ref.shape[0]):
        out_ref[dest] = packed


def final_kernel(recv_ref, sigma_ref, basis_ref, ritz_ref, out_ref):
    total = recv_ref[0]
    for source in range(1, recv_ref.shape[0]):
        total = total + recv_ref[source]
    nb = ritz_ref.shape[0]
    moments = jnp.concatenate([total[:, :nb], total[:, nb : 2 * nb]], axis=0)
    gram = jnp.concatenate([total[:, 2 * nb : 3 * nb], total[:, 3 * nb :]], axis=0)
    ritz = ritz_ref[...]
    dot = functools.partial(jnp.dot, precision=HIGH, preferred_element_type=jnp.float32)
    first = moments - dot(gram, ritz)
    second = first - dot(gram, first)
    weights = ritz + first + second
    out_ref[...] = sigma_ref[...] - lax.dot_general(
        weights, basis_ref[...], TN, precision=HIGH, preferred_element_type=jnp.float32
    )


def shape(*dims, dtype=jnp.float32):
    return jax.ShapeDtypeStruct(dims, dtype)


def call(kernel, outs, ins, operands, scratch=()):
    single = not isinstance(outs, tuple)
    return pl.pallas_call(
        kernel,
        out_shape=outs,
        in_specs=ins,
        out_specs=VMEM if single else (VMEM,) * len(outs),
        scratch_shapes=list(scratch),
        compiler_params=pltpu.CompilerParams(vmem_limit_bytes=16 * 1024 * 1024),
    )(*operands)


def per_device(n_row, n_col, blocks, block_cols, block_slot, trials, basis, ritz_terms):
    local = blocks[0]
    rows, per_row, size, _ = local.shape
    stored, vectors, _ = trials.shape[1:]
    nb, chunk = basis.shape
    cols = jnp.transpose(block_cols, (1, 0, 2))
    local, owned, cols_hbm, table_hbm, basis_hbm = (
        pltpu.with_memory_space_constraint(value, pltpu.HBM)
        for value in (local, trials[0], cols, block_slot, basis)
    )
    half = nb // 2

    requests, packed, owned = call(
        request_kernel,
        (
            shape(n_row * REQUEST_ROWS, LANES, dtype=jnp.int32),
            shape(1, half, LANES),
            shape(stored, vectors, size),
        ),
        [HBM, HBM, HBM, HBM],
        (cols_hbm, table_hbm, basis_hbm, owned),
        [
            pltpu.SMEM(cols.shape, jnp.int32),
            pltpu.SMEM(block_slot.shape, jnp.int32),
            pltpu.VMEM(basis.shape, jnp.float32),
            pltpu.SemaphoreType.DMA((4,)),
        ],
    )
    wanted = lax.all_to_all(requests, "row", 0, 0, tiled=True)

    def neighbour(value, step):
        return lax.ppermute(value, "col", [(i, i ^ step) for i in range(n_col)])

    def join(left, right):
        return call(join_kernel, shape(2 * left.shape[0], half, LANES), [VMEM, VMEM], (left, right))

    for step in STEPS[:EARLY]:
        other = neighbour(packed, step)
        if step == STEPS[EARLY - 1]:
            break
        packed = join(packed, other)
    sent = call(pick_kernel, shape(n_row, vectors, size), [VMEM, VMEM], (wanted, owned))
    sent, other = lax.optimization_barrier((sent, other))
    chosen = lax.all_to_all(sent, "row", 0, 0, tiled=True)
    packed = join(packed, other)
    for step in STEPS[EARLY:]:
        packed = join(packed, neighbour(packed, step))
    held = 1
    early = call(
        load_kernel, shape(held, per_row, size, size), [HBM], (local,), [pltpu.SemaphoreType.DMA]
    )
    row_basis = call(basis_kernel, shape(nb, n_col * chunk), [VMEM], (packed,))
    gram = call(gram_kernel, shape(nb, nb), [VMEM], (row_basis,))

    partial_sums = call(
        functools.partial(partial_kernel, stored),
        shape(n_col, half + half // 2, LANES),
        [SMEM, SMEM, VMEM, HBM, VMEM, VMEM],
        (cols, block_slot, early, local, chosen, row_basis),
        [
            pltpu.VMEM((vectors, rows * size), jnp.float32),
            pltpu.VMEM((rows - held, per_row, size, size), jnp.float32),
            pltpu.SemaphoreType.DMA((rows - held,)),
        ],
    )
    gathered = lax.all_to_all(partial_sums, "col", 0, 0, tiled=True)
    sigma, keep, moments = call(
        sum_kernel,
        (shape(vectors, chunk), shape(vectors, chunk), shape(n_row, half, LANES)),
        [VMEM, VMEM],
        (gathered, gram),
    )
    all_moments = lax.all_to_all(moments, "row", 0, 0, tiled=True)
    corrections = call(
        final_kernel,
        shape(vectors, chunk),
        [VMEM, VMEM, VMEM, VMEM],
        (all_moments, keep, basis, ritz_terms),
    )
    return sigma, corrections


def solution(mesh):
    in_specs = (
        P("col", "row", None, None, None),
        P("col", "row", None),
        P("col", None),
        P("col", "row", None, None),
        P(None, ("row", "col")),
        P(),
    )
    out_specs = (P(None, ("row", "col")), P(None, ("row", "col")))
    body = functools.partial(per_device, mesh.shape["row"], mesh.shape["col"])
    return jax.shard_map(body, mesh=mesh, in_specs=in_specs, out_specs=out_specs, check_vma=False)
```

time: 111 us -> 110 us (level)
  starting transfers between devices: 29.6 us -> 56 us
  blocking collectives: 34.2 us -> 20.1 us
  waiting for transfers between devices: 30.1 us -> 21.1 us
  local copies, waits for them, and re-layouts: 6.58 us -> 0.02 us
  Pallas kernels: 7.68 us -> 10.9 us
  other arithmetic: 1.61 us -> 0 us
    ppermute x0 -> x4, starting transfers between devices: none -> 24.8 us  [neighbour(): return lax.ppermute(value, 'col', [(i, i ^ step) for i in range(n_col)])]
    all_to_all x1 -> x0, blocking collectives: 17 us -> none  [per_device(): gathered = lax.all_to_all(partial_sums, 'col', 0, 0, tiled=True)]
    all_to_all x1, waiting for transfers between devices: 15.7 us -> 2.05 us  [per_device(): chosen = lax.all_to_all(sent, 'row', 0, 0, tiled=True)]
    ppermute x0 -> x4, waiting for transfers between devices: none -> 6.95 us  [neighbour(): return lax.ppermute(value, 'col', [(i, i ^ step) for i in range(n_col)])]
    all_to_all x1, waiting for transfers between devices: 5.34 us -> 0.01 us  [per_device(): wanted = lax.all_to_all(requests, 'row', 0, 0, tiled=True)]
    unnamed x16 -> x8, local copies, waits for them, and re-layouts: 5.25 us -> 0.02 us
    pallas_call x5 -> x12, Pallas kernels: 7.68 us -> 10.9 us  [call(): pl.pallas_call(kernel, out_shape=outs, in_specs=ins, out_specs=VMEM if si...]
    all_to_all x1, waiting for transfers between devices: 9.09 us -> 12.1 us  [per_device(): gathered = lax.all_to_all(partial_sums, 'col', 0, 0, tiled=True)]
  transfers between devices with their start and end apart: 3 -> 7, of which waited for: 3 -> 5; matrix products, arithmetic and copies ran while one was open for 3% -> 0% of each run, Pallas kernels for 2% -> 3%
where the time goes in v2:
time: 110 us; the launch traced here: 109 us
  starting transfers between devices  56 us (51%)
  waiting for transfers between devices  21.1 us (19%)
  blocking collectives  20.1 us (18%)
  Pallas kernels  10.9 us (10%)
    ppermute x4, starting transfers between devices, neighbour(): return lax.ppermute(value, 'col', [(i, i ^ step) for i in range(n_col)])  24.8 us
    all_to_all x1, blocking collectives, per_device(): all_moments = lax.all_to_all(moments, 'row', 0, 0, tiled=True)  20.1 us
    all_to_all x1, waiting for transfers between devices, per_device(): gathered = lax.all_to_all(partial_sums, 'col', 0, 0, tiled=True)  12.1 us
    all_to_all x1, starting transfers between devices, per_device(): gathered = lax.all_to_all(partial_sums, 'col', 0, 0, tiled=True)  11.8 us
    pallas_call x12, Pallas kernels, call(): pl.pallas_call(kernel, out_shape=outs, in_specs=ins, out_specs=VMEM if si...  10.9 us
    all_to_all x1, starting transfers between devices, per_device(): wanted = lax.all_to_all(requests, 'row', 0, 0, tiled=True)  10.4 us
    all_to_all x1, starting transfers between devices, per_device(): chosen = lax.all_to_all(sent, 'row', 0, 0, tiled=True)  9.02 us
    ppermute x4, waiting for transfers between devices, neighbour(): return lax.ppermute(value, 'col', [(i, i ^ step) for i in range(n_col)])  6.95 us
  transfers between devices with their start and end apart: 7, of which 5 were waited for; matrix products, arithmetic and copies ran while one was open for 0% of the time, Pallas kernels for 3%

profile of v2, /device:TPU:1, one launch (start us, length us, event | category | flops | bytes accessed | tf_op | source)
XLA Modules:
  0.0 109.0 jit_solution(9824488755361983625)
XLA Ops:
  0.6 1.6 %shard_map.78 = (s32[64,128]{1,0:T(8,128)}, f32[1,16,128]{2,1,0:T(8,128)S(1)}, f32[6,32,256]{2,1,0:T(8,128)S(1)}) custom-call(s32[3,1,4]{2,1,0:T(1,128)} %bitcast.6, s32[1,192]{1,0:T(1,128)} %table_ref.1, f32[32,48]{1,0:T(8,128)} %basis_ref.1, f32[6,32,256]{2,1,0:T(8,128)} %bitcast.10), custom_call_target="tpu_custom_call" | custom-call | tf_op jit(solution)/shard_map/pallas_call | solution.py:190
  2.2 10.4 %all-to-all-start = ((s32[32,2,128]{2,1,0:T(2,128)}), s32[32,2,128]{2,1,0:T(2,128)S(1)}, u32[]{:S(2)}, u32[]{:S(2)}) async-start(s32[32,2,128]{2,1,0:T(2,128)} %bitcast.3), calls=%async_computation | async-start | bytes 65536 | tf_op jit(solution)/shard_map/all_to_all | solution.py:228
  12.6 1.9 %collective-permute-start = (f32[1,16,128]{2,1,0:T(8,128)S(1)}, f32[1,16,128]{2,1,0:T(8,128)S(1)}, u32[]{:S(2)}, u32[]{:S(2)}) collective-permute-start(f32[1,16,128]{2,1,0:T(8,128)S(1)} %get-tuple-element.12.left_ref), channel_id=1, source_target_pairs={{0,1},{1,0},{2,3},{3,2},{4,5},{5,4},{6,7},{7,6},{8,9},{9,8},{10,11... | collective-permute-start | bytes 24584 | tf_op jit(solution)/shard_map/ppermute | solution.py:231
  14.5 2.8 %collective-permute-done.right_ref = f32[1,16,128]{2,1,0:T(8,128)S(1)} collective-permute-done((f32[1,16,128]{2,1,0:T(8,128)S(1)}, f32[1,16,128]{2,1,0:T(8,128)S(1)}, u32[]{:S(2)}, u32[]{:S(2)}) %collective-permute-start) | collective-permute-done | bytes 8224 | tf_op jit(solution)/shard_map/ppermute | solution.py:231
  17.3 13.7 %collective-permute-start.1 = (f32[2,16,128]{2,1,0:T(8,128)S(1)}, f32[2,16,128]{2,1,0:T(8,128)S(1)}, u32[]{:S(2)}, u32[]{:S(2)}) collective-permute-start(f32[2,16,128]{2,1,0:T(8,128)S(1)} %shard_map.80.left_ref), channel_id=1, source_target_pairs={{0,8},{1,9},{2,10},{3,11},{4,12},{5,13},{6,14},{7,15},{8,0},{9,1},... | collective-permute-start | bytes 49160 | tf_op jit(solution)/shard_map/ppermute | solution.py:231
  31.0 0.0 all-to-all-done
  31.0 1.2 %shard_map.79 = f32[32,32,256]{2,1,0:T(8,128)} custom-call(s32[64,128]{1,0:T(8,128)S(1)} %bitcast.5, f32[6,32,256]{2,1,0:T(8,128)S(1)} %get-tuple-element.11.trials_ref), custom_call_target="tpu_custom_call" | custom-call | tf_op jit(solution)/shard_map/pallas_call | solution.py:190
  32.1 0.0 copy-start.2
  32.2 0.0 copy-start.3
  32.2 0.0 collective-permute-done.1.right_ref
  32.2 9.0 %all-to-all-start.1 = ((f32[32,32,256]{2,1,0:T(8,128)}), f32[32,32,256]{2,1,0:T(8,128)S(1)}, u32[]{:S(2)}, u32[]{:S(2)}) async-start(f32[32,32,256]{2,1,0:T(8,128)} %shard_map.79), calls=%async_computation.1 | async-start | bytes 2097152 | tf_op jit(solution)/shard_map/all_to_all | solution.py:243
  41.2 5.8 %collective-permute-start.2 = (f32[4,16,128]{2,1,0:T(8,128)S(1)}, f32[4,16,128]{2,1,0:T(8,128)S(1)}, u32[]{:S(2)}, u32[]{:S(2)}) collective-permute-start(f32[4,16,128]{2,1,0:T(8,128)S(1)} %shard_map.81.left_ref), channel_id=1, source_target_pairs={{0,4},{1,5},{2,6},{3,7},{4,0},{5,1},{6,2},{7,3},{8,12},{9,13},{10,... | collective-permute-start | bytes 98312 | tf_op jit(solution)/shard_map/ppermute | solution.py:231
  47.0 3.0 %collective-permute-done.2.right_ref = f32[4,16,128]{2,1,0:T(8,128)S(1)} collective-permute-done((f32[4,16,128]{2,1,0:T(8,128)S(1)}, f32[4,16,128]{2,1,0:T(8,128)S(1)}, u32[]{:S(2)}, u32[]{:S(2)}) %collective-permute-start.2) | collective-permute-done | bytes 32800 | tf_op jit(solution)/shard_map/ppermute | solution.py:231
  49.9 3.4 %collective-permute-start.3 = (f32[8,16,128]{2,1,0:T(8,128)S(1)}, f32[8,16,128]{2,1,0:T(8,128)S(1)}, u32[]{:S(2)}, u32[]{:S(2)}) collective-permute-start(f32[8,16,128]{2,1,0:T(8,128)S(1)} %shard_map.82.left_ref), channel_id=1, source_target_pairs={{0,2},{1,3},{2,0},{3,1},{4,6},{5,7},{6,4},{7,5},{8,10},{9,11},{10,... | collective-permute-start | bytes 196616 | tf_op jit(solution)/shard_map/ppermute | solution.py:231
  53.4 1.2 %shard_map.77.held_ref = f32[1,4,256,256]{3,2,1,0:T(8,128)S(1)} custom-call(f32[3,4,256,256]{3,2,1,0:T(8,128)} %bitcast.8), custom_call_target="tpu_custom_call" | custom-call | tf_op jit(solution)/shard_map/pallas_call | solution.py:190
  54.6 1.2 %collective-permute-done.3.right_ref = f32[8,16,128]{2,1,0:T(8,128)S(1)} collective-permute-done((f32[8,16,128]{2,1,0:T(8,128)S(1)}, f32[8,16,128]{2,1,0:T(8,128)S(1)}, u32[]{:S(2)}, u32[]{:S(2)}) %collective-permute-start.3) | collective-permute-done | bytes 65568 | tf_op jit(solution)/shard_map/ppermute | solution.py:231
  55.8 0.4 shard_map.84.basis_ref
  56.3 0.0 copy-start
  56.3 0.0 copy-start.1
  56.3 2.1 %all-to-all-done.1.chosen_ref = f32[32,32,256]{2,1,0:T(8,128)S(1)} async-done(((f32[32,32,256]{2,1,0:T(8,128)}), f32[32,32,256]{2,1,0:T(8,128)S(1)}, u32[]{:S(2)}, u32[]{:S(2)}) %all-to-all-start.1) | async-done | bytes 1048608 | tf_op jit(solution)/shard_map/all_to_all | solution.py:243
  58.4 0.0 copy-done.2
  58.4 0.0 copy-done.3
  58.4 4.2 %shard_map.85 = f32[16,24,128]{2,1,0:T(8,128)} custom-call(s32[3,1,4]{2,1,0:T(1,128)S(1)} %bitcast.7, s32[1,192]{1,0:T(1,128)S(1)} %copy-done.3, f32[1,4,256,256]{3,2,1,0:T(8,128)S(1)} %shard_map.77.held_ref, f32[3,4,256,256]{3,2,1,0:T(8,128)} %bitcast.9, f32[32,32,256]{2,1,0:T(8,128)S(1)} %all-to-all-done.1.chosen_ref, f32[32,768]{1,0:T(8,128)S(1)} %shard_map.84.basis_ref), custom_call_target="tpu_custom_call" | custom-call | tf_op jit(solution)/shard_map/pallas_call | solution.py:190
  62.6 11.8 %all-to-all-start.2 = ((f32[16,24,128]{2,1,0:T(8,128)}), f32[16,24,128]{2,1,0:T(8,128)S(1)}, u32[]{:S(2)}, u32[]{:S(2)}) async-start(f32[16,24,128]{2,1,0:T(8,128)} %shard_map.85), calls=%async_computation.2 | async-start | bytes 393216 | tf_op jit(solution)/shard_map/all_to_all | solution.py:265
  74.5 0.2 shard_map.86.gram_ref
  74.7 12.1 %all-to-all-done.2.recv_ref = f32[16,24,128]{2,1,0:T(8,128)S(1)} async-done(((f32[16,24,128]{2,1,0:T(8,128)}), f32[16,24,128]{2,1,0:T(8,128)S(1)}, u32[]{:S(2)}, u32[]{:S(2)}) %all-to-all-start.2) | async-done | bytes 196640 | tf_op jit(solution)/shard_map/all_to_all | solution.py:265
  86.8 0.7 shard_map.87
  87.5 20.1 %all_to_all.26.recv_ref = f32[32,16,128]{2,1,0:T(8,128)S(1)} all-to-all(f32[32,16,128]{2,1,0:T(8,128)S(1)} %get-tuple-element.16), channel_id=1, replica_groups=mesh['row'=32,'col'=16] {'row'}, dimensions={0} | all-to-all | bytes 524288 | tf_op jit(solution)/shard_map/all_to_all | solution.py:272
  107.7 0.0 copy-done
  107.7 0.0 copy-done.1
  107.7 1.3 %shard_map.88 = f32[32,48]{1,0:T(8,128)} custom-call(f32[32,16,128]{2,1,0:T(8,128)S(1)} %all_to_all.26.recv_ref, f32[32,48]{1,0:T(8,128)S(1)} %get-tuple-element.17.sigma_ref, f32[32,48]{1,0:T(8,128)S(1)} %copy-done, f32[32,32]{1,0:T(8,128)S(1)} %copy-done.1), custom_call_target="tpu_custom_call" | custom-call | tf_op jit(solution)/shard_map/pallas_call | solution.py:190
  (4 shorter events, 0.0 us)
Async XLA Ops:
  2.2 28.7 %all-to-all-start = ((s32[32,2,128]{2,1,0:T(2,128)}), s32[32,2,128]{2,1,0:T(2,128)S(1)}, u32[]{:S(2)}, u32[]{:S(2)}) async-start(s32[32,2,128]{2,1,0:T(2,128)} %bitcast.3), calls=%async_computation | async-start | bytes 65536 | tf_op jit(solution)/shard_map/all_to_all | solution.py:228
  12.6 4.7 %collective-permute-start = (f32[1,16,128]{2,1,0:T(8,128)S(1)}, f32[1,16,128]{2,1,0:T(8,128)S(1)}, u32[]{:S(2)}, u32[]{:S(2)}) collective-permute-start(f32[1,16,128]{2,1,0:T(8,128)S(1)} %get-tuple-element.12.left_ref), channel_id=1, source_target_pairs={{0,1},{1,0},{2,3},{3,2},{4,5},{5,4},{6,7},{7,6},{8,9},{9,8},{10,11... | collective-permute-start | bytes 24584 | tf_op jit(solution)/shard_map/ppermute | solution.py:231
  17.3 14.9 %collective-permute-start.1 = (f32[2,16,128]{2,1,0:T(8,128)S(1)}, f32[2,16,128]{2,1,0:T(8,128)S(1)}, u32[]{:S(2)}, u32[]{:S(2)}) collective-permute-start(f32[2,16,128]{2,1,0:T(8,128)S(1)} %shard_map.80.left_ref), channel_id=1, source_target_pairs={{0,8},{1,9},{2,10},{3,11},{4,12},{5,13},{6,14},{7,15},{8,0},{9,1},... | collective-permute-start | bytes 49160 | tf_op jit(solution)/shard_map/ppermute | solution.py:231
  32.1 26.2 %copy-start.2 = (s32[1,3,4]{2,0,1:T(1,128)S(1)}, s32[1,3,4]{2,0,1:T(1,128)}, u32[]{:S(2)}) copy-start(s32[1,3,4]{2,0,1:T(1,128)} %param.7) | copy-start | bytes 148
  32.2 26.2 %copy-start.3 = (s32[1,192]{1,0:T(1,128)S(1)}, s32[1,192]{1,0:T(1,128)}, u32[]{:S(2)}) copy-start(s32[1,192]{1,0:T(1,128)} %table_ref.1) | copy-start | bytes 2308
  32.2 26.2 %all-to-all-start.1 = ((f32[32,32,256]{2,1,0:T(8,128)}), f32[32,32,256]{2,1,0:T(8,128)S(1)}, u32[]{:S(2)}, u32[]{:S(2)}) async-start(f32[32,32,256]{2,1,0:T(8,128)} %shard_map.79), calls=%async_computation.1 | async-start | bytes 2097152 | tf_op jit(solution)/shard_map/all_to_all | solution.py:243
  41.2 8.7 %collective-permute-start.2 = (f32[4,16,128]{2,1,0:T(8,128)S(1)}, f32[4,16,128]{2,1,0:T(8,128)S(1)}, u32[]{:S(2)}, u32[]{:S(2)}) collective-permute-start(f32[4,16,128]{2,1,0:T(8,128)S(1)} %shard_map.81.left_ref), channel_id=1, source_target_pairs={{0,4},{1,5},{2,6},{3,7},{4,0},{5,1},{6,2},{7,3},{8,12},{9,13},{10,... | collective-permute-start | bytes 98312 | tf_op jit(solution)/shard_map/ppermute | solution.py:231
  49.9 5.9 %collective-permute-start.3 = (f32[8,16,128]{2,1,0:T(8,128)S(1)}, f32[8,16,128]{2,1,0:T(8,128)S(1)}, u32[]{:S(2)}, u32[]{:S(2)}) collective-permute-start(f32[8,16,128]{2,1,0:T(8,128)S(1)} %shard_map.82.left_ref), channel_id=1, source_target_pairs={{0,2},{1,3},{2,0},{3,1},{4,6},{5,7},{6,4},{7,5},{8,10},{9,11},{10,... | collective-permute-start | bytes 196616 | tf_op jit(solution)/shard_map/ppermute | solution.py:231
  56.3 51.4 %copy-start = (f32[32,48]{1,0:T(8,128)S(1)}, f32[32,48]{1,0:T(8,128)}, u32[]{:S(2)}) copy-start(f32[32,48]{1,0:T(8,128)} %basis_ref.1) | copy-start | bytes 18436
  56.3 51.4 %copy-start.1 = (f32[32,32]{1,0:T(8,128)S(1)}, f32[32,32]{1,0:T(8,128)}, u32[]{:S(2)}) copy-start(f32[32,32]{1,0:T(8,128)} %ritz_ref.1) | copy-start | bytes 12292
  62.6 24.2 %all-to-all-start.2 = ((f32[16,24,128]{2,1,0:T(8,128)}), f32[16,24,128]{2,1,0:T(8,128)S(1)}, u32[]{:S(2)}, u32[]{:S(2)}) async-start(f32[16,24,128]{2,1,0:T(8,128)} %shard_map.85), calls=%async_computation.2 | async-start | bytes 393216 | tf_op jit(solution)/shard_map/all_to_all | solution.py:265

commit v3 on v2

v3 whole, which is shorter than its diff:
```python
import functools

import jax
import jax.numpy as jnp
from jax import lax
from jax.experimental import pallas as pl
from jax.experimental.pallas import tpu as pltpu
from jax.sharding import PartitionSpec as P

LANES = 128
HIGH = lax.Precision.HIGHEST
SMEM = pl.BlockSpec(memory_space=pltpu.SMEM)
VMEM = pl.BlockSpec(memory_space=pltpu.VMEM)
HBM = pl.BlockSpec(memory_space=pltpu.HBM)
NT = (((1,), (1,)), ((), ()))
TN = (((0,), (0,)), ((), ()))
CORES = 2
PACKED = 12


def pack(value):
    quarters = [value[8 * i : 8 * i + 8] for i in range(4)]
    cut = LANES - 2 * value.shape[1]
    upper = jnp.concatenate([quarters[0], quarters[1], quarters[2][:, :cut]], axis=1)
    rest = jnp.concatenate([quarters[2][:, cut:], quarters[3]], axis=1)
    return jnp.concatenate([upper, jnp.concatenate([rest[:4], rest[4:]], axis=1)], axis=0)


def unpack(rows, chunk):
    cut = LANES - 2 * chunk
    upper = rows[:8]
    rest = jnp.concatenate([rows[8:, : LANES // 2], rows[8:, LANES // 2 :]], axis=0)
    third = jnp.concatenate([upper[:, 2 * chunk :], rest[:, : chunk - cut]], axis=1)
    return jnp.concatenate(
        [upper[:, :chunk], upper[:, chunk : 2 * chunk], third, rest[:, chunk - cut :]], axis=0
    )


def put_rows(out_ref, group, start, rows):
    for row in range(rows.shape[0]):
        here = slice((start + row) * LANES, (start + row + 1) * LANES)
        out_ref[group, :, here] = rows[row : row + 1]


def slot_of(cols_ref, table_ref, row, entry):
    return table_ref[0, cols_ref[row, 0, entry]]


def spread_kernel(basis_ref, out_ref):
    packed = pack(basis_ref[...])
    for dest in range(out_ref.shape[0]):
        put_rows(out_ref, dest, 0, packed)


def request_kernel(cols_hbm, table_hbm, out_ref, cols, table, sems, *, stored):
    copies = [
        pltpu.make_async_copy(source, target, sems.at[index])
        for index, (source, target) in enumerate([(cols_hbm, cols), (table_hbm, table)])
    ]
    for copy in copies:
        copy.start()
    for copy in copies:
        copy.wait()
    owners = lax.broadcasted_iota(jnp.int32, out_ref.shape, 0)
    wanted = jnp.zeros(out_ref.shape, jnp.int32)
    for row in range(cols.shape[0]):
        for entry in range(cols.shape[2]):
            slot = slot_of(cols, table, row, entry)
            owner = slot // stored
            wanted = jnp.where(owners == owner, slot - owner * stored, wanted)
    out_ref[...] = wanted


def pick_kernel(wanted_ref, own_hbm, other_hbm, out_ref, pair, sems):
    dests, vectors, size = out_ref.shape
    stored = own_hbm.shape[0]
    core = lax.axis_index("row") % CORES
    copies = [
        pltpu.make_async_copy(own_hbm, pair.at[core], sems.at[0]),
        pltpu.make_async_copy(other_hbm, pair.at[1 - core], sems.at[1]),
    ]
    for copy in copies:
        copy.start()
    for copy in copies:
        copy.wait()
    for dest in range(dests):
        owner = dest % CORES
        want = jnp.broadcast_to(wanted_ref[dest : dest + 1, :], (8, LANES))
        masks = [want == index for index in range(1, stored)]
        for top in range(0, vectors, 8):
            for left in range(0, size, LANES):
                here = (slice(top, top + 8), slice(left, left + LANES))
                tile = pair[owner, 0, *here]
                for index in range(1, stored):
                    tile = jnp.where(masks[index - 1], pair[owner, index, *here], tile)
                out_ref[dest, *here] = tile


def split(value):
    top = value.astype(jnp.bfloat16)
    rest = (value - top.astype(jnp.float32)).astype(jnp.bfloat16)
    return top, rest


def basis_kernel(packed_ref, out_ref, rows):
    groups = packed_ref.shape[0]
    chunk = out_ref.shape[1] // groups
    for group in range(groups):
        for row in range(PACKED):
            rows[row : row + 1] = packed_ref[group, :, row * LANES : (row + 1) * LANES]
        out_ref[:, group * chunk : (group + 1) * chunk] = unpack(rows[:PACKED], chunk)


def gram_kernel(basis_ref, out_ref):
    basis = basis_ref[...]
    out_ref[...] = lax.dot_general(basis, basis, NT, precision=HIGH, preferred_element_type=jnp.float32)


def partial_kernel(stored, cols_ref, table_ref, blocks_ref, chosen_ref, basis_ref, out_ref, part):
    rows, per_row, size, _ = blocks_ref.shape
    vectors = chosen_ref.shape[1]
    groups = out_ref.shape[0]
    for row in range(rows):
        total = jnp.zeros((vectors, size), jnp.float32)
        for entry in range(per_row):
            owner = slot_of(cols_ref, table_ref, row, entry) // stored
            vec_top, vec_rest = split(chosen_ref[owner])
            mat_top, mat_rest = split(blocks_ref[row, entry])
            both = jnp.concatenate([vec_top, vec_rest], axis=0)
            first = lax.dot_general(both, mat_top, NT, preferred_element_type=jnp.float32)
            second = lax.dot_general(vec_top, mat_rest, NT, preferred_element_type=jnp.float32)
            total += first[:vectors] + (first[vectors:] + second)
        part[:, row * size : (row + 1) * size] = total
    moments = lax.dot_general(
        basis_ref[...], part[...], NT, precision=HIGH, preferred_element_type=jnp.float32
    )
    quarter = vectors // 4
    chunk = rows * size // groups
    tail = jnp.concatenate([moments[i * quarter : (i + 1) * quarter] for i in range(4)], axis=1)
    for group in range(groups):
        put_rows(out_ref, group, 0, pack(part[:, group * chunk : (group + 1) * chunk]))
        put_rows(out_ref, group, PACKED, tail)


def sum_kernel(recv_ref, gram_ref, sigma_ref, keep_ref, out_ref, rows):
    vectors, chunk = sigma_ref.shape
    half, quarter = vectors // 2, vectors // 4
    for row in range(PACKED + quarter):
        here = slice(row * LANES, (row + 1) * LANES)
        total = recv_ref[0, :, here]
        for group in range(1, recv_ref.shape[0]):
            total = total + recv_ref[group, :, here]
        place = row if row < PACKED else row - PACKED + 16
        rows[place : place + 1] = total
    sigma = unpack(rows[:PACKED], chunk)
    sigma_ref[...] = sigma
    keep_ref[...] = sigma
    tail = rows[16 : 16 + quarter]
    moments = jnp.concatenate([tail[:, i * vectors : (i + 1) * vectors] for i in range(4)], axis=0)
    gram = gram_ref[...]
    packed = jnp.concatenate([moments[:half], moments[half:], gram[:half], gram[half:]], axis=1)
    for dest in range(out_ref.shape[0]):
        out_ref[dest] = packed


def final_kernel(recv_ref, sigma_ref, basis_ref, ritz_ref, out_ref):
    total = recv_ref[0]
    for source in range(1, recv_ref.shape[0]):
        total = total + recv_ref[source]
    nb = ritz_ref.shape[0]
    moments = jnp.concatenate([total[:, :nb], total[:, nb : 2 * nb]], axis=0)
    gram = jnp.concatenate([total[:, 2 * nb : 3 * nb], total[:, 3 * nb :]], axis=0)
    ritz = ritz_ref[...]
    dot = functools.partial(jnp.dot, precision=HIGH, preferred_element_type=jnp.float32)
    first = moments - dot(gram, ritz)
    second = first - dot(gram, first)
    weights = ritz + first + second
    out_ref[...] = sigma_ref[...] - lax.dot_general(
        weights, basis_ref[...], TN, precision=HIGH, preferred_element_type=jnp.float32
    )


def shape(*dims, dtype=jnp.float32):
    return jax.ShapeDtypeStruct(dims, dtype)


def call(kernel, outs, ins, operands, scratch=()):
    single = not isinstance(outs, tuple)
    return pl.pallas_call(
        kernel,
        out_shape=outs,
        in_specs=ins,
        out_specs=VMEM if single else (VMEM,) * len(outs),
        scratch_shapes=list(scratch),
        compiler_params=pltpu.CompilerParams(vmem_limit_bytes=16 * 1024 * 1024),
    )(*operands)


def per_device(n_row, n_col, blocks, block_cols, block_slot, trials, basis, ritz_terms):
    local = blocks[0]
    rows, per_row, size, _ = local.shape
    owned = trials[0]
    stored, vectors, _ = owned.shape
    nb, chunk = basis.shape
    cols = jnp.transpose(block_cols, (1, 0, 2))
    half, quarter = nb // 2, nb // 4
    in_hbm = functools.partial(pltpu.with_memory_space_constraint, memory_space=pltpu.HBM)
    quarter = nb // 4
    groups = [list(range(core, n_row, CORES)) for core in range(CORES)]

    packed = call(spread_kernel, shape(n_col, 1, nb * chunk), [VMEM], (basis,))
    packed = lax.all_to_all(packed, "col", 0, 0, tiled=True)
    owned = in_hbm(owned)
    other = lax.ppermute(owned, "row", [(i, i ^ 1) for i in range(n_row)])
    requests = call(
        functools.partial(request_kernel, stored=stored),
        shape(n_row, LANES, dtype=jnp.int32),
        [HBM, HBM],
        (in_hbm(cols), in_hbm(block_slot)),
        [
            pltpu.SMEM(cols.shape, jnp.int32),
            pltpu.SMEM(block_slot.shape, jnp.int32),
            pltpu.SemaphoreType.DMA((2,)),
        ],
    )
    requests, packed, other = lax.optimization_barrier((requests, packed, other))
    wanted = lax.all_to_all(requests, "row", 0, 0, tiled=True, axis_index_groups=groups)
    row_basis = call(
        basis_kernel,
        shape(nb, n_col * chunk),
        [VMEM],
        (packed,),
        [pltpu.VMEM((16, LANES), jnp.float32)],
    )
    gram = call(gram_kernel, shape(nb, nb), [VMEM], (row_basis,))
    sent = call(
        pick_kernel,
        shape(n_row, vectors, size),
        [VMEM, HBM, HBM],
        (wanted, owned, in_hbm(other)),
        [pltpu.VMEM((CORES, stored, vectors, size), jnp.float32), pltpu.SemaphoreType.DMA((2,))],
    )
    sent, local, row_basis, gram = lax.optimization_barrier((sent, local, row_basis, gram))
    chosen = lax.all_to_all(sent, "row", 0, 0, tiled=True, axis_index_groups=groups)

    partial_sums = call(
        functools.partial(partial_kernel, stored),
        shape(n_col, 1, (PACKED + quarter) * LANES),
        [SMEM, SMEM, VMEM, VMEM, VMEM],
        (cols, block_slot, local, chosen, row_basis),
        [pltpu.VMEM((vectors, rows * size), jnp.float32)],
    )
    gathered = lax.all_to_all(partial_sums, "col", 0, 0, tiled=True)
    sigma, keep, moments = call(
        sum_kernel,
        (shape(vectors, chunk), shape(vectors, chunk), shape(n_row, half, LANES)),
        [VMEM, VMEM],
        (gathered, gram),
        [pltpu.VMEM((24, LANES), jnp.float32)],
    )
    all_moments = lax.all_to_all(moments, "row", 0, 0, tiled=True)
    corrections = call(
        final_kernel,
        shape(vectors, chunk),
        [VMEM, VMEM, VMEM, VMEM],
        (all_moments, keep, basis, ritz_terms),
    )
    return sigma, corrections


def solution(mesh):
    in_specs = (
        P("col", "row", None, None, None),
        P("col", "row", None),
        P("col", None),
        P("col", "row", None, None),
        P(None, ("row", "col")),
        P(),
    )
    out_specs = (P(None, ("row", "col")), P(None, ("row", "col")))
    body = functools.partial(per_device, mesh.shape["row"], mesh.shape["col"])
    return jax.shard_map(body, mesh=mesh, in_specs=in_specs, out_specs=out_specs, check_vma=False)
```

time: 110 us -> 100 us (0.909)
  blocking collectives: 20.1 us -> 51.4 us
  starting transfers between devices: 56 us -> 25.4 us
  waiting for transfers between devices: 21.1 us -> 13.4 us
  Pallas kernels: 10.9 us -> 8.11 us
    all_to_all x0 -> x2, blocking collectives: none -> 34.4 us  [the longest x1 18.6 us: per_device(): gathered = lax.all_to_all(partial_sums, 'col', 0, 0, tiled=True)]
    ppermute x4 -> x1, starting transfers between devices: 24.8 us -> 2.87 us  [per_device(): other = lax.ppermute(owned, 'row', [(i, i ^ 1) for i in range(n_row)])]
    all_to_all x3 -> x2, starting transfers between devices: 31.2 us -> 22.5 us  [the longest x1 15.7 us: per_device(): packed = lax.all_to_all(packed, 'col', 0, 0, tiled=True)]
    ppermute x4 -> x1, waiting for transfers between devices: 6.95 us -> 0.01 us  [per_device(): other = lax.ppermute(owned, 'row', [(i, i ^ 1) for i in range(n_row)])]
    all_to_all x1, blocking collectives: 20.1 us -> 17 us  [per_device(): all_moments = lax.all_to_all(moments, 'row', 0, 0, tiled=True)]
    pallas_call x12 -> x8, Pallas kernels: 10.9 us -> 8.11 us  [call(): pl.pallas_call(kernel, out_shape=outs, in_specs=ins, out_specs=VMEM if si...]
    all_to_all x3 -> x2, waiting for transfers between devices: 14.2 us -> 13.4 us  [the longest x1 7.55 us: per_device(): packed = lax.all_to_all(packed, 'col', 0, 0, tiled=True)]
  transfers between devices with their start and end apart: 7 -> 3, of which waited for: 5 -> 2; matrix products, arithmetic and copies ran while one was open for 0% -> 0% of each run, Pallas kernels for 3% -> 2%
where the time goes in v3:
time: 100 us; the launch traced here: 99.9 us
  blocking collectives  51.4 us (51%)
  starting transfers between devices  25.4 us (25%)
  waiting for transfers between devices  13.4 us (13%)
  Pallas kernels  8.11 us (8%)
    all_to_all x1, blocking collectives, per_device(): gathered = lax.all_to_all(partial_sums, 'col', 0, 0, tiled=True)  18.6 us
    all_to_all x1, blocking collectives, per_device(): all_moments = lax.all_to_all(moments, 'row', 0, 0, tiled=True)  17 us
    all_to_all x1, starting transfers between devices, per_device(): packed = lax.all_to_all(packed, 'col', 0, 0, tiled=True)  15.7 us
    all_to_all x1, blocking collectives, per_device(): lax.all_to_all(sent, 'row', 0, 0, tiled=True, axis_index_groups=groups)  15.7 us
    pallas_call x8, Pallas kernels, call(): pl.pallas_call(kernel, out_shape=outs, in_specs=ins, out_specs=VMEM if si...  8.11 us
    all_to_all x1, waiting for transfers between devices, per_device(): packed = lax.all_to_all(packed, 'col', 0, 0, tiled=True)  7.55 us
    all_to_all x1, starting transfers between devices, per_device(): lax.all_to_all(requests, 'row', 0, 0, tiled=True, axis_index_groups=groups)  6.76 us
    all_to_all x1, waiting for transfers between devices, per_device(): lax.all_to_all(requests, 'row', 0, 0, tiled=True, axis_index_groups=groups)  5.9 us
  transfers between devices with their start and end apart: 3, of which 2 were waited for; matrix products, arithmetic and copies ran while one was open for 0% of the time, Pallas kernels for 2%

profile of v3, /device:TPU:1, one launch (start us, length us, event | category | flops | bytes accessed | tf_op | source)
XLA Modules:
  0.0 99.9 jit_solution(6934840763464777634)
XLA Ops:
  0.6 0.0 copy-start
  0.6 0.0 copy-start.1
  0.7 0.9 copy-done.1
  1.5 0.0 copy-start.4
  1.5 0.0 copy-start.5
  1.5 0.8 shard_map.78
  2.3 15.7 %all-to-all-start = ((f32[16,1,1536]{2,1,0:T(1,128)}), f32[16,1,1536]{2,1,0:T(1,128)S(1)}, u32[]{:S(2)}, u32[]{:S(2)}) async-start(f32[16,1,1536]{2,1,0:T(1,128)} %shard_map.78), calls=%async_computation | async-start | bytes 196608 | tf_op jit(solution)/shard_map/all_to_all | solution.py:212
  18.1 2.9 %collective-permute-start = (f32[6,32,256]{2,1,0:T(8,128)}, f32[6,32,256]{2,1,0:T(8,128)}, u32[]{:S(2)}, u32[]{:S(2)}) collective-permute-start(f32[6,32,256]{2,1,0:T(8,128)} %bitcast.9), channel_id=1, source_target_pairs={{0,16},{16,0},{32,48},{48,32},{64,80},{80,64},{96,112},{112,96},{1... | collective-permute-start | bytes 589832 | tf_op jit(solution)/shard_map/ppermute | solution.py:214
  20.9 1.4 %shard_map.77 = s32[32,128]{1,0:T(8,128)} custom-call(s32[3,1,4]{2,1,0:T(1,128)} %bitcast.7, s32[1,192]{1,0:T(1,128)} %table_ref.1), custom_call_target="tpu_custom_call" | custom-call | tf_op jit(solution)/shard_map/pallas_call | solution.py:189
  22.4 0.0 collective-permute-done.other_hbm
  22.4 7.5 %all-to-all-done.packed_ref = f32[16,1,1536]{2,1,0:T(1,128)S(1)} async-done(((f32[16,1,1536]{2,1,0:T(1,128)}), f32[16,1,1536]{2,1,0:T(1,128)S(1)}, u32[]{:S(2)}, u32[]{:S(2)}) %all-to-all-start) | async-done | bytes 98336 | tf_op jit(solution)/shard_map/all_to_all | solution.py:212
  29.9 6.8 %all-to-all-start.1 = ((s32[16,2,128]{2,1,0:T(2,128)}), s32[16,2,128]{2,1,0:T(2,128)S(1)}, u32[]{:S(2)}, u32[]{:S(2)}) async-start(s32[16,2,128]{2,1,0:T(2,128)} %bitcast.2), calls=%async_computation.1 | async-start | bytes 32768 | tf_op jit(solution)/shard_map/all_to_all | solution.py:227
  36.7 0.3 shard_map.80.basis_ref
  37.0 0.2 shard_map.81.gram_ref
  37.2 5.9 %all-to-all-done.1 = s32[16,2,128]{2,1,0:T(2,128)S(1)} async-done(((s32[16,2,128]{2,1,0:T(2,128)}), s32[16,2,128]{2,1,0:T(2,128)S(1)}, u32[]{:S(2)}, u32[]{:S(2)}) %all-to-all-start.1) | async-done | bytes 16416 | tf_op jit(solution)/shard_map/all_to_all | solution.py:227
  43.1 1.3 %shard_map.79 = f32[32,32,256]{2,1,0:T(8,128)S(1)} custom-call(s32[32,128]{1,0:T(8,128)S(1)} %bitcast.6, f32[6,32,256]{2,1,0:T(8,128)} %bitcast.10, f32[6,32,256]{2,1,0:T(8,128)} %collective-permute-done.other_hbm), custom_call_target="tpu_custom_call" | custom-call | tf_op jit(solution)/shard_map/pallas_call | solution.py:189
  44.4 15.7 %all_to_all.31.chosen_ref = f32[32,32,256]{2,1,0:T(8,128)S(1)} all-to-all(f32[32,32,256]{2,1,0:T(8,128)S(1)} %shard_map.79), channel_id=1, replica_groups={{0,32,64,96,128,160,192,224,256,288,320,352,384,416,448,480},{16,48,80,..., dimensions={0} | all-to-all | bytes 2097152 | tf_op jit(solution)/shard_map/all_to_all | solution.py:244
  60.2 0.0 copy-done
  60.2 0.0 copy-done.4
  60.2 0.0 copy-done.5
  60.2 0.0 copy-start.2
  60.2 0.0 copy-start.3
  60.2 2.0 %shard_map.82 = f32[16,1,2560]{2,1,0:T(1,128)S(1)} custom-call(s32[3,1,4]{2,1,0:T(1,128)S(1)} %bitcast.8, s32[1,192]{1,0:T(1,128)S(1)} %copy-done.5, f32[3,4,256,256]{3,2,1,0:T(8,128)S(1)} %bitcast.5, f32[32,32,256]{2,1,0:T(8,128)S(1)} %all_to_all.31.chosen_ref, f32[32,768]{1,0:T(8,128)S(1)} %shard_map.80.basis_ref), custom_call_target="tpu_custom_call" | custom-call | tf_op jit(solution)/shard_map/pallas_call | solution.py:189
  62.2 18.6 %all_to_all.32.recv_ref = f32[16,1,2560]{2,1,0:T(1,128)S(1)} all-to-all(f32[16,1,2560]{2,1,0:T(1,128)S(1)} %shard_map.82), channel_id=1, replica_groups=mesh['row'=32,'col'=16] {'col'}, dimensions={0} | all-to-all | bytes 327680 | tf_op jit(solution)/shard_map/all_to_all | solution.py:253
  80.8 0.8 shard_map.83
  81.6 17.0 %all_to_all.33.recv_ref = f32[32,16,128]{2,1,0:T(8,128)S(1)} all-to-all(f32[32,16,128]{2,1,0:T(8,128)S(1)} %get-tuple-element.20), channel_id=1, replica_groups=mesh['row'=32,'col'=16] {'row'}, dimensions={0} | all-to-all | bytes 524288 | tf_op jit(solution)/shard_map/all_to_all | solution.py:261
  98.6 0.0 copy-done.2
  98.6 0.0 copy-done.3
  98.6 1.3 %shard_map.84 = f32[32,48]{1,0:T(8,128)} custom-call(f32[32,16,128]{2,1,0:T(8,128)S(1)} %all_to_all.33.recv_ref, f32[32,48]{1,0:T(8,128)S(1)} %get-tuple-element.21.sigma_ref, f32[32,48]{1,0:T(8,128)S(1)} %copy-done.2, f32[32,32]{1,0:T(8,128)S(1)} %copy-done.3), custom_call_target="tpu_custom_call" | custom-call | tf_op jit(solution)/shard_map/pallas_call | solution.py:189
Async XLA Ops:
  0.6 59.5 %copy-start = (f32[1,3,4,256,256]{4,3,2,1,0:T(8,128)S(1)}, f32[1,3,4,256,256]{4,3,2,1,0:T(8,128)}, u32[]{:S(2)}) copy-start(f32[1,3,4,256,256]{4,3,2,1,0:T(8,128)} %param.6) | copy-start | bytes 9437188
  0.6 0.9 copy-start.1
  1.5 58.6 %copy-start.4 = (s32[1,3,4]{2,0,1:T(1,128)S(1)}, s32[1,3,4]{2,0,1:T(1,128)}, u32[]{:S(2)}) copy-start(s32[1,3,4]{2,0,1:T(1,128)} %param.7) | copy-start | bytes 148
  1.5 58.7 %copy-start.5 = (s32[1,192]{1,0:T(1,128)S(1)}, s32[1,192]{1,0:T(1,128)}, u32[]{:S(2)}) copy-start(s32[1,192]{1,0:T(1,128)} %table_ref.1) | copy-start | bytes 2308
  2.3 27.6 %all-to-all-start = ((f32[16,1,1536]{2,1,0:T(1,128)}), f32[16,1,1536]{2,1,0:T(1,128)S(1)}, u32[]{:S(2)}, u32[]{:S(2)}) async-start(f32[16,1,1536]{2,1,0:T(1,128)} %shard_map.78), calls=%async_computation | async-start | bytes 196608 | tf_op jit(solution)/shard_map/all_to_all | solution.py:212
  18.1 4.3 %collective-permute-start = (f32[6,32,256]{2,1,0:T(8,128)}, f32[6,32,256]{2,1,0:T(8,128)}, u32[]{:S(2)}, u32[]{:S(2)}) collective-permute-start(f32[6,32,256]{2,1,0:T(8,128)} %bitcast.9), channel_id=1, source_target_pairs={{0,16},{16,0},{32,48},{48,32},{64,80},{80,64},{96,112},{112,96},{1... | collective-permute-start | bytes 589832 | tf_op jit(solution)/shard_map/ppermute | solution.py:214
  29.9 13.2 %all-to-all-start.1 = ((s32[16,2,128]{2,1,0:T(2,128)}), s32[16,2,128]{2,1,0:T(2,128)S(1)}, u32[]{:S(2)}, u32[]{:S(2)}) async-start(s32[16,2,128]{2,1,0:T(2,128)} %bitcast.2), calls=%async_computation.1 | async-start | bytes 32768 | tf_op jit(solution)/shard_map/all_to_all | solution.py:227
  60.2 38.5 %copy-start.2 = (f32[32,48]{1,0:T(8,128)S(1)}, f32[32,48]{1,0:T(8,128)}, u32[]{:S(2)}) copy-start(f32[32,48]{1,0:T(8,128)} %basis_ref.3) | copy-start | bytes 18436
  60.2 38.5 %copy-start.3 = (f32[32,32]{1,0:T(8,128)S(1)}, f32[32,32]{1,0:T(8,128)}, u32[]{:S(2)}) copy-start(f32[32,32]{1,0:T(8,128)} %ritz_ref.1) | copy-start | bytes 12292

commit v4 on v3

--- a/solution.py
+++ b/solution.py
@@ -16,6 +16,8 @@
 TN = (((0,), (0,)), ((), ()))
 CORES = 2
 PACKED = 12
+COL_FIRST = 8
+ROW_FIRST = 20
 
 
 def pack(value):
@@ -61,7 +63,7 @@
         copy.start()
     for copy in copies:
         copy.wait()
-    owners = lax.broadcasted_iota(jnp.int32, out_ref.shape, 0)
+    owners = (lax.broadcasted_iota(jnp.int32, out_ref.shape, 0) + ROW_FIRST) % out_ref.shape[0]
     wanted = jnp.zeros(out_ref.shape, jnp.int32)
     for row in range(cols.shape[0]):
         for entry in range(cols.shape[2]):
@@ -106,8 +108,9 @@
     groups = packed_ref.shape[0]
     chunk = out_ref.shape[1] // groups
     for group in range(groups):
+        place = (group - COL_FIRST) % groups
         for row in range(PACKED):
-            rows[row : row + 1] = packed_ref[group, :, row * LANES : (row + 1) * LANES]
+            rows[row : row + 1] = packed_ref[place, :, row * LANES : (row + 1) * LANES]
         out_ref[:, group * chunk : (group + 1) * chunk] = unpack(rows[:PACKED], chunk)
 
 
@@ -124,7 +127,8 @@
         total = jnp.zeros((vectors, size), jnp.float32)
         for entry in range(per_row):
             owner = slot_of(cols_ref, table_ref, row, entry) // stored
-            vec_top, vec_rest = split(chosen_ref[owner])
+            place = (owner + chosen_ref.shape[0] - ROW_FIRST) % chosen_ref.shape[0]
+            vec_top, vec_rest = split(chosen_ref[place])
             mat_top, mat_rest = split(blocks_ref[row, entry])
             both = jnp.concatenate([vec_top, vec_rest], axis=0)
             first = lax.dot_general(both, mat_top, NT, preferred_element_type=jnp.float32)
@@ -138,8 +142,9 @@
     chunk = rows * size // groups
     tail = jnp.concatenate([moments[i * quarter : (i + 1) * quarter] for i in range(4)], axis=1)
     for group in range(groups):
-        put_rows(out_ref, group, 0, pack(part[:, group * chunk : (group + 1) * chunk]))
-        put_rows(out_ref, group, PACKED, tail)
+        place = (group - COL_FIRST) % groups
+        put_rows(out_ref, place, 0, pack(part[:, group * chunk : (group + 1) * chunk]))
+        put_rows(out_ref, place, PACKED, tail)
 
 
 def sum_kernel(recv_ref, gram_ref, sigma_ref, keep_ref, out_ref, rows):
@@ -196,6 +201,10 @@
     )(*operands)
 
 
+def turned(count, first):
+    return [(first + index) % count for index in range(count)]
+
+
 def per_device(n_row, n_col, blocks, block_cols, block_slot, trials, basis, ritz_terms):
     local = blocks[0]
     rows, per_row, size, _ = local.shape
@@ -206,10 +215,12 @@
     half, quarter = nb // 2, nb // 4
     in_hbm = functools.partial(pltpu.with_memory_space_constraint, memory_space=pltpu.HBM)
     quarter = nb // 4
-    groups = [list(range(core, n_row, CORES)) for core in range(CORES)]
+    whole_col = [turned(n_col, COL_FIRST)]
+    whole_row = [turned(n_row, ROW_FIRST)]
+    groups = [[row for row in whole_row[0] if row % CORES == core] for core in range(CORES)]
 
     packed = call(spread_kernel, shape(n_col, 1, nb * chunk), [VMEM], (basis,))
-    packed = lax.all_to_all(packed, "col", 0, 0, tiled=True)
+    packed = lax.all_to_all(packed, "col", 0, 0, tiled=True, axis_index_groups=whole_col)
     owned = in_hbm(owned)
     other = lax.ppermute(owned, "row", [(i, i ^ 1) for i in range(n_row)])
     requests = call(
@@ -250,7 +261,7 @@
         (cols, block_slot, local, chosen, row_basis),
         [pltpu.VMEM((vectors, rows * size), jnp.float32)],
     )
-    gathered = lax.all_to_all(partial_sums, "col", 0, 0, tiled=True)
+    gathered = lax.all_to_all(partial_sums, "col", 0, 0, tiled=True, axis_index_groups=whole_col)
     sigma, keep, moments = call(
         sum_kernel,
         (shape(vectors, chunk), shape(vectors, chunk), shape(n_row, half, LANES)),
@@ -258,7 +269,7 @@
         (gathered, gram),
         [pltpu.VMEM((24, LANES), jnp.float32)],
     )
-    all_moments = lax.all_to_all(moments, "row", 0, 0, tiled=True)
+    all_moments = lax.all_to_all(moments, "row", 0, 0, tiled=True, axis_index_groups=whole_row)
     corrections = call(
         final_kernel,
         shape(vectors, chunk),

time: 100 us -> 93 us (0.930)
  waiting for transfers between devices: 13.4 us -> 1.84 us
  starting transfers between devices: 25.4 us -> 30.9 us
  blocking collectives: 51.4 us -> 50 us
    all_to_all x1, waiting for transfers between devices: 7.55 us -> 0.55 us  [per_device(): lax.all_to_all(packed, 'col', 0, 0, tiled=True, axis_index_groups=whole_col)]
    all_to_all x1, waiting for transfers between devices: 5.9 us -> 1.28 us  [per_device(): lax.all_to_all(requests, 'row', 0, 0, tiled=True, axis_index_groups=groups)]
    all_to_all x2, blocking collectives: 35.7 us -> 32 us  [the longest x1 16.5 us: per_device(): lax.all_to_all(partial_sums, 'col', 0, 0, tiled=True, axis_index_groups=w...]
    all_to_all x1, starting transfers between devices: 15.7 us -> 19.1 us  [per_device(): lax.all_to_all(packed, 'col', 0, 0, tiled=True, axis_index_groups=whole_col)]
    all_to_all x1, blocking collectives: 15.7 us -> 18 us  [per_device(): lax.all_to_all(sent, 'row', 0, 0, tiled=True, axis_index_groups=groups)]
    all_to_all x1, starting transfers between devices: 6.76 us -> 8.69 us  [per_device(): lax.all_to_all(requests, 'row', 0, 0, tiled=True, axis_index_groups=groups)]
where the time goes in v4:
time: 93 us; the launch traced here: 92.5 us
  blocking collectives  50 us (54%)
  starting transfers between devices  30.9 us (33%)
  Pallas kernels  8.1 us (9%)
  waiting for transfers between devices  1.84 us (2%)
    all_to_all x1, starting transfers between devices, per_device(): lax.all_to_all(packed, 'col', 0, 0, tiled=True, axis_index_groups=whole_col)  19.1 us
    all_to_all x1, blocking collectives, per_device(): lax.all_to_all(sent, 'row', 0, 0, tiled=True, axis_index_groups=groups)  18 us
    all_to_all x1, blocking collectives, per_device(): lax.all_to_all(partial_sums, 'col', 0, 0, tiled=True, axis_index_groups=w...  16.5 us
    all_to_all x1, blocking collectives, per_device(): lax.all_to_all(moments, 'row', 0, 0, tiled=True, axis_index_groups=whole_...  15.5 us
    all_to_all x1, starting transfers between devices, per_device(): lax.all_to_all(requests, 'row', 0, 0, tiled=True, axis_index_groups=groups)  8.69 us
    pallas_call x8, Pallas kernels, call(): pl.pallas_call(kernel, out_shape=outs, in_specs=ins, out_specs=VMEM if si...  8.1 us
    ppermute x1, starting transfers between devices, per_device(): other = lax.ppermute(owned, 'row', [(i, i ^ 1) for i in range(n_row)])  3.13 us
  transfers between devices with their start and end apart: 3, of which 2 were waited for; matrix products, arithmetic and copies ran while one was open for 0% of the time, Pallas kernels for 2%

profile of v4, /device:TPU:1, one launch (start us, length us, event | category | flops | bytes accessed | tf_op | source)
XLA Modules:
  0.0 92.5 jit_solution(16704192671836518054)
XLA Ops:
  0.6 0.0 copy-start
  0.6 0.0 copy-start.1
  0.7 0.9 copy-done.1
  1.5 0.0 copy-start.4
  1.5 0.0 copy-start.5
  1.5 0.8 shard_map.78
  2.3 19.1 %all-to-all-start = ((f32[16,1,1536]{2,1,0:T(1,128)}), f32[16,1,1536]{2,1,0:T(1,128)S(1)}, u32[]{:S(2)}, u32[]{:S(2)}) async-start(f32[16,1,1536]{2,1,0:T(1,128)} %shard_map.78), calls=%async_computation | async-start | bytes 196608 | tf_op jit(solution)/shard_map/all_to_all | solution.py:223
  21.4 3.1 %collective-permute-start = (f32[6,32,256]{2,1,0:T(8,128)}, f32[6,32,256]{2,1,0:T(8,128)}, u32[]{:S(2)}, u32[]{:S(2)}) collective-permute-start(f32[6,32,256]{2,1,0:T(8,128)} %bitcast.9), channel_id=1, source_target_pairs={{0,16},{16,0},{32,48},{48,32},{64,80},{80,64},{96,112},{112,96},{1... | collective-permute-start | bytes 589832 | tf_op jit(solution)/shard_map/ppermute | solution.py:225
  24.6 1.4 %shard_map.77 = s32[32,128]{1,0:T(8,128)} custom-call(s32[3,1,4]{2,1,0:T(1,128)} %bitcast.7, s32[1,192]{1,0:T(1,128)} %table_ref.1), custom_call_target="tpu_custom_call" | custom-call | tf_op jit(solution)/shard_map/pallas_call | solution.py:194
  26.0 0.0 collective-permute-done.other_hbm
  26.0 0.6 all-to-all-done.packed_ref
  26.6 8.7 %all-to-all-start.1 = ((s32[16,2,128]{2,1,0:T(2,128)}), s32[16,2,128]{2,1,0:T(2,128)S(1)}, u32[]{:S(2)}, u32[]{:S(2)}) async-start(s32[16,2,128]{2,1,0:T(2,128)} %bitcast.2), calls=%async_computation.1 | async-start | bytes 32768 | tf_op jit(solution)/shard_map/all_to_all | solution.py:238
  35.2 0.3 shard_map.80.basis_ref
  35.6 0.2 shard_map.81.gram_ref
  35.8 1.3 %all-to-all-done.1 = s32[16,2,128]{2,1,0:T(2,128)S(1)} async-done(((s32[16,2,128]{2,1,0:T(2,128)}), s32[16,2,128]{2,1,0:T(2,128)S(1)}, u32[]{:S(2)}, u32[]{:S(2)}) %all-to-all-start.1) | async-done | bytes 16416 | tf_op jit(solution)/shard_map/all_to_all | solution.py:238
  37.1 1.3 %shard_map.79 = f32[32,32,256]{2,1,0:T(8,128)S(1)} custom-call(s32[32,128]{1,0:T(8,128)S(1)} %bitcast.6, f32[6,32,256]{2,1,0:T(8,128)} %bitcast.10, f32[6,32,256]{2,1,0:T(8,128)} %collective-permute-done.other_hbm), custom_call_target="tpu_custom_call" | custom-call | tf_op jit(solution)/shard_map/pallas_call | solution.py:194
  38.4 18.0 %all_to_all.31.chosen_ref = f32[32,32,256]{2,1,0:T(8,128)S(1)} all-to-all(f32[32,32,256]{2,1,0:T(8,128)S(1)} %shard_map.79), channel_id=1, replica_groups={{320,352,384,416,448,480,0,32,64,96,128,160,192,224,256,288},{336,368,4..., dimensions={0} | all-to-all | bytes 2097152 | tf_op jit(solution)/shard_map/all_to_all | solution.py:255
  56.4 0.0 copy-done
  56.4 0.0 copy-done.4
  56.4 0.0 copy-done.5
  56.4 0.0 copy-start.2
  56.4 0.0 copy-start.3
  56.5 2.0 %shard_map.82 = f32[16,1,2560]{2,1,0:T(1,128)S(1)} custom-call(s32[3,1,4]{2,1,0:T(1,128)S(1)} %bitcast.8, s32[1,192]{1,0:T(1,128)S(1)} %copy-done.5, f32[3,4,256,256]{3,2,1,0:T(8,128)S(1)} %bitcast.5, f32[32,32,256]{2,1,0:T(8,128)S(1)} %all_to_all.31.chosen_ref, f32[32,768]{1,0:T(8,128)S(1)} %shard_map.80.basis_ref), custom_call_target="tpu_custom_call" | custom-call | tf_op jit(solution)/shard_map/pallas_call | solution.py:194
  58.4 16.5 %all_to_all.32.recv_ref = f32[16,1,2560]{2,1,0:T(1,128)S(1)} all-to-all(f32[16,1,2560]{2,1,0:T(1,128)S(1)} %shard_map.82), channel_id=1, replica_groups={{8,9,10,11,12,13,14,15,0,1,2,3,4,5,6,7},{24,25,26,27,28,29,30,31,16,17,..., dimensions={0} | all-to-all | bytes 327680 | tf_op jit(solution)/shard_map/all_to_all | solution.py:264
  74.9 0.8 shard_map.83
  75.7 15.5 %all_to_all.33.recv_ref = f32[32,16,128]{2,1,0:T(8,128)S(1)} all-to-all(f32[32,16,128]{2,1,0:T(8,128)S(1)} %get-tuple-element.20), channel_id=1, replica_groups={{320,336,352,368,384,400,416,432,448,464,480,496,0,16,32,48,64,80,96,11..., dimensions={0} | all-to-all | bytes 524288 | tf_op jit(solution)/shard_map/all_to_all | solution.py:272
  91.2 0.0 copy-done.2
  91.2 0.0 copy-done.3
  91.2 1.3 %shard_map.84 = f32[32,48]{1,0:T(8,128)} custom-call(f32[32,16,128]{2,1,0:T(8,128)S(1)} %all_to_all.33.recv_ref, f32[32,48]{1,0:T(8,128)S(1)} %get-tuple-element.21.sigma_ref, f32[32,48]{1,0:T(8,128)S(1)} %copy-done.2, f32[32,32]{1,0:T(8,128)S(1)} %copy-done.3), custom_call_target="tpu_custom_call" | custom-call | tf_op jit(solution)/shard_map/pallas_call | solution.py:194
Async XLA Ops:
  0.6 55.8 %copy-start = (f32[1,3,4,256,256]{4,3,2,1,0:T(8,128)S(1)}, f32[1,3,4,256,256]{4,3,2,1,0:T(8,128)}, u32[]{:S(2)}) copy-start(f32[1,3,4,256,256]{4,3,2,1,0:T(8,128)} %param.6) | copy-start | bytes 9437188
  0.6 0.9 copy-start.1
  1.5 54.9 %copy-start.4 = (s32[1,3,4]{2,0,1:T(1,128)S(1)}, s32[1,3,4]{2,0,1:T(1,128)}, u32[]{:S(2)}) copy-start(s32[1,3,4]{2,0,1:T(1,128)} %param.7) | copy-start | bytes 148
  1.5 54.9 %copy-start.5 = (s32[1,192]{1,0:T(1,128)S(1)}, s32[1,192]{1,0:T(1,128)}, u32[]{:S(2)}) copy-start(s32[1,192]{1,0:T(1,128)} %table_ref.1) | copy-start | bytes 2308
  2.3 24.2 %all-to-all-start = ((f32[16,1,1536]{2,1,0:T(1,128)}), f32[16,1,1536]{2,1,0:T(1,128)S(1)}, u32[]{:S(2)}, u32[]{:S(2)}) async-start(f32[16,1,1536]{2,1,0:T(1,128)} %shard_map.78), calls=%async_computation | async-start | bytes 196608 | tf_op jit(solution)/shard_map/all_to_all | solution.py:223
  21.4 4.6 %collective-permute-start = (f32[6,32,256]{2,1,0:T(8,128)}, f32[6,32,256]{2,1,0:T(8,128)}, u32[]{:S(2)}, u32[]{:S(2)}) collective-permute-start(f32[6,32,256]{2,1,0:T(8,128)} %bitcast.9), channel_id=1, source_target_pairs={{0,16},{16,0},{32,48},{48,32},{64,80},{80,64},{96,112},{112,96},{1... | collective-permute-start | bytes 589832 | tf_op jit(solution)/shard_map/ppermute | solution.py:225
  26.6 10.5 %all-to-all-start.1 = ((s32[16,2,128]{2,1,0:T(2,128)}), s32[16,2,128]{2,1,0:T(2,128)S(1)}, u32[]{:S(2)}, u32[]{:S(2)}) async-start(s32[16,2,128]{2,1,0:T(2,128)} %bitcast.2), calls=%async_computation.1 | async-start | bytes 32768 | tf_op jit(solution)/shard_map/all_to_all | solution.py:238
  56.4 34.8 %copy-start.2 = (f32[32,48]{1,0:T(8,128)S(1)}, f32[32,48]{1,0:T(8,128)}, u32[]{:S(2)}) copy-start(f32[32,48]{1,0:T(8,128)} %basis_ref.3) | copy-start | bytes 18436
  56.4 34.8 %copy-start.3 = (f32[32,32]{1,0:T(8,128)S(1)}, f32[32,32]{1,0:T(8,128)}, u32[]{:S(2)}) copy-start(f32[32,32]{1,0:T(8,128)} %ritz_ref.1) | copy-start | bytes 12292

commit v5 on v4

--- a/solution.py
+++ b/solution.py
@@ -16,7 +16,7 @@
 TN = (((0,), (0,)), ((), ()))
 CORES = 2
 PACKED = 12
-COL_FIRST = 8
+COL_FIRST = 10
 ROW_FIRST = 20
 
 
@@ -73,9 +73,7 @@
     out_ref[...] = wanted
 
 
-def pick_kernel(wanted_ref, own_hbm, other_hbm, out_ref, pair, sems):
-    dests, vectors, size = out_ref.shape
-    stored = own_hbm.shape[0]
+def pair_kernel(own_hbm, other_hbm, pair, sems):
     core = lax.axis_index("row") % CORES
     copies = [
         pltpu.make_async_copy(own_hbm, pair.at[core], sems.at[0]),
@@ -85,6 +83,11 @@
         copy.start()
     for copy in copies:
         copy.wait()
+
+
+def pick_kernel(wanted_ref, pair, out_ref):
+    dests, vectors, size = out_ref.shape
+    stored = pair.shape[1]
     for dest in range(dests):
         owner = dest % CORES
         want = jnp.broadcast_to(wanted_ref[dest : dest + 1, :], (8, LANES))
@@ -177,12 +180,13 @@
     gram = jnp.concatenate([total[:, 2 * nb : 3 * nb], total[:, 3 * nb :]], axis=0)
     ritz = ritz_ref[...]
     dot = functools.partial(jnp.dot, precision=HIGH, preferred_element_type=jnp.float32)
+    turn = functools.partial(
+        lax.dot_general, dimension_numbers=TN, precision=HIGH, preferred_element_type=jnp.float32
+    )
+    basis = basis_ref[...]
     first = moments - dot(gram, ritz)
-    second = first - dot(gram, first)
-    weights = ritz + first + second
-    out_ref[...] = sigma_ref[...] - lax.dot_general(
-        weights, basis_ref[...], TN, precision=HIGH, preferred_element_type=jnp.float32
-    )
+    both = 2.0 * basis - turn(gram, basis)
+    out_ref[...] = (sigma_ref[...] - turn(ritz, basis)) - turn(first, both)
 
 
 def shape(*dims, dtype=jnp.float32):
@@ -244,13 +248,14 @@
         [pltpu.VMEM((16, LANES), jnp.float32)],
     )
     gram = call(gram_kernel, shape(nb, nb), [VMEM], (row_basis,))
-    sent = call(
-        pick_kernel,
-        shape(n_row, vectors, size),
-        [VMEM, HBM, HBM],
-        (wanted, owned, in_hbm(other)),
-        [pltpu.VMEM((CORES, stored, vectors, size), jnp.float32), pltpu.SemaphoreType.DMA((2,))],
-    )
+    pair = call(
+        pair_kernel,
+        shape(CORES, stored, vectors, size),
+        [HBM, HBM],
+        (owned, in_hbm(other)),
+        [pltpu.SemaphoreType.DMA((2,))],
+    )
+    sent = call(pick_kernel, shape(n_row, vectors, size), [VMEM, VMEM], (wanted, pair))
     sent, local, row_basis, gram = lax.optimization_barrier((sent, local, row_basis, gram))
     chosen = lax.all_to_all(sent, "row", 0, 0, tiled=True, axis_index_groups=groups)
 

time: 93 us -> 91.4 us (0.983)
  starting transfers between devices: 30.9 us -> 29.1 us
  local copies, waits for them, and re-layouts: 0.89 us -> 2.14 us
    all_to_all x1, blocking collectives: 18 us -> 16.1 us  [per_device(): lax.all_to_all(sent, 'row', 0, 0, tiled=True, axis_index_groups=groups)]
    all_to_all x1, starting transfers between devices: 19.1 us -> 17.3 us  [per_device(): lax.all_to_all(packed, 'col', 0, 0, tiled=True, axis_index_groups=whole_col)]
    all_to_all x1, waiting for transfers between devices: 1.28 us -> 0.01 us  [per_device(): lax.all_to_all(requests, 'row', 0, 0, tiled=True, axis_index_groups=groups)]
    all_to_all x1, waiting for transfers between devices: 0.55 us -> 1.82 us  [per_device(): lax.all_to_all(packed, 'col', 0, 0, tiled=True, axis_index_groups=whole_col)]
    unnamed x12 -> x20, local copies, waits for them, and re-layouts: 0.89 us -> 2.14 us
    pallas_call x8 -> x9, Pallas kernels: 8.1 us -> 7.95 us  [call(): pl.pallas_call(kernel, out_shape=outs, in_specs=ins, out_specs=VMEM if si...]
  transfers between devices with their start and end apart: 3 -> 3, of which waited for: 2 -> 1; matrix products, arithmetic and copies ran while one was open for 0% -> 0% of each run, Pallas kernels for 2% -> 3%
where the time goes in v5:
time: 91.4 us; the launch traced here: 90.9 us
  blocking collectives  49.1 us (54%)
  starting transfers between devices  29.1 us (32%)
  Pallas kernels  7.95 us (9%)
  local copies, waits for them, and re-layouts  2.14 us (2%)
  waiting for transfers between devices  1.83 us (2%)
    all_to_all x1, starting transfers between devices, per_device(): lax.all_to_all(packed, 'col', 0, 0, tiled=True, axis_index_groups=whole_col)  17.3 us
    all_to_all x1, blocking collectives, per_device(): lax.all_to_all(partial_sums, 'col', 0, 0, tiled=True, axis_index_groups=w...  17.2 us
    all_to_all x1, blocking collectives, per_device(): lax.all_to_all(sent, 'row', 0, 0, tiled=True, axis_index_groups=groups)  16.1 us
    all_to_all x1, blocking collectives, per_device(): lax.all_to_all(moments, 'row', 0, 0, tiled=True, axis_index_groups=whole_...  15.7 us
    all_to_all x1, starting transfers between devices, per_device(): lax.all_to_all(requests, 'row', 0, 0, tiled=True, axis_index_groups=groups)  8.69 us
    pallas_call x9, Pallas kernels, call(): pl.pallas_call(kernel, out_shape=outs, in_specs=ins, out_specs=VMEM if si...  7.95 us
    ppermute x1, starting transfers between devices, per_device(): other = lax.ppermute(owned, 'row', [(i, i ^ 1) for i in range(n_row)])  3.13 us
    unnamed x20, local copies, waits for them, and re-layouts  2.14 us
  transfers between devices with their start and end apart: 3, of which 1 were waited for; matrix products, arithmetic and copies ran while one was open for 0% of the time, Pallas kernels for 3%

profile of v5, /device:TPU:1, one launch (start us, length us, event | category | flops | bytes accessed | tf_op | source)
XLA Modules:
  0.0 90.9 jit_solution(1646269858859715720)
XLA Ops:
  0.6 0.0 copy-start
  0.6 0.0 copy-start.3
  0.7 0.9 copy-done.3
  1.5 0.8 shard_map.78
  2.3 17.3 %all-to-all-start = ((f32[16,1,1536]{2,1,0:T(1,128)}), f32[16,1,1536]{2,1,0:T(1,128)S(1)}, u32[]{:S(2)}, u32[]{:S(2)}) async-start(f32[16,1,1536]{2,1,0:T(1,128)} %shard_map.78), calls=%async_computation | async-start | bytes 196608 | tf_op jit(solution)/shard_map/all_to_all | solution.py:227
  19.6 3.1 %collective-permute-start = (f32[6,32,256]{2,1,0:T(8,128)}, f32[6,32,256]{2,1,0:T(8,128)}, u32[]{:S(2)}, u32[]{:S(2)}) collective-permute-start(f32[6,32,256]{2,1,0:T(8,128)} %bitcast.9), channel_id=1, source_target_pairs={{0,16},{16,0},{32,48},{48,32},{64,80},{80,64},{96,112},{112,96},{1... | collective-permute-start | bytes 589832 | tf_op jit(solution)/shard_map/ppermute | solution.py:229
  22.8 1.4 %shard_map.77 = s32[32,128]{1,0:T(8,128)} custom-call(s32[3,1,4]{2,1,0:T(1,128)} %bitcast.7, s32[1,192]{1,0:T(1,128)} %table_ref.1), custom_call_target="tpu_custom_call" | custom-call | tf_op jit(solution)/shard_map/pallas_call | solution.py:198
  24.2 0.0 collective-permute-done.other_hbm
  24.2 1.8 %all-to-all-done.packed_ref = f32[16,1,1536]{2,1,0:T(1,128)S(1)} async-done(((f32[16,1,1536]{2,1,0:T(1,128)}), f32[16,1,1536]{2,1,0:T(1,128)S(1)}, u32[]{:S(2)}, u32[]{:S(2)}) %all-to-all-start) | async-done | bytes 98336 | tf_op jit(solution)/shard_map/all_to_all | solution.py:227
  26.0 8.7 %all-to-all-start.1 = ((s32[16,2,128]{2,1,0:T(2,128)}), s32[16,2,128]{2,1,0:T(2,128)S(1)}, u32[]{:S(2)}, u32[]{:S(2)}) async-start(s32[16,2,128]{2,1,0:T(2,128)} %bitcast.2), calls=%async_computation.1 | async-start | bytes 32768 | tf_op jit(solution)/shard_map/all_to_all | solution.py:242
  34.7 0.3 shard_map.81.basis_ref
  35.0 0.2 shard_map.82.gram_ref
  35.2 0.6 copy-done.1
  35.9 0.6 copy-done.5
  36.5 1.0 %shard_map.79.pair = f32[2,6,32,256]{3,2,1,0:T(8,128)S(1)} custom-call(f32[6,32,256]{2,1,0:T(8,128)} %bitcast.10, f32[6,32,256]{2,1,0:T(8,128)} %collective-permute-done.other_hbm), custom_call_target="tpu_custom_call" | custom-call | tf_op jit(solution)/shard_map/pallas_call | solution.py:198
  37.5 0.0 all-to-all-done.1
  37.5 0.0 copy-start.2
  37.5 0.0 copy-start.8
  37.6 0.0 copy-start.9
  37.6 0.3 shard_map.80
  37.8 0.0 copy-start.6
  37.9 16.1 %all_to_all.31.chosen_ref = f32[32,32,256]{2,1,0:T(8,128)S(1)} all-to-all(f32[32,32,256]{2,1,0:T(8,128)S(1)} %shard_map.80), channel_id=1, replica_groups={{320,352,384,416,448,480,0,32,64,96,128,160,192,224,256,288},{336,368,4..., dimensions={0} | all-to-all | bytes 2097152 | tf_op jit(solution)/shard_map/all_to_all | solution.py:260
  54.0 0.0 copy-done
  54.0 0.0 copy-done.2
  54.0 0.0 copy-done.8
  54.0 0.0 copy-start.4
  54.0 0.0 copy-start.7
  54.0 2.0 %shard_map.83 = f32[16,1,2560]{2,1,0:T(1,128)S(1)} custom-call(s32[3,1,4]{2,1,0:T(1,128)S(1)} %bitcast.8, s32[1,192]{1,0:T(1,128)S(1)} %copy-done.9, f32[3,4,256,256]{3,2,1,0:T(8,128)S(1)} %bitcast.5, f32[32,32,256]{2,1,0:T(8,128)S(1)} %all_to_all.31.chosen_ref, f32[32,768]{1,0:T(8,128)S(1)} %copy-done.2), custom_call_target="tpu_custom_call" | custom-call | tf_op jit(solution)/shard_map/pallas_call | solution.py:198
  56.0 17.2 %all_to_all.32.recv_ref = f32[16,1,2560]{2,1,0:T(1,128)S(1)} all-to-all(f32[16,1,2560]{2,1,0:T(1,128)S(1)} %shard_map.83), channel_id=1, replica_groups={{10,11,12,13,14,15,0,1,2,3,4,5,6,7,8,9},{26,27,28,29,30,31,16,17,18,19,..., dimensions={0} | all-to-all | bytes 327680 | tf_op jit(solution)/shard_map/all_to_all | solution.py:269
  73.2 0.8 shard_map.84
  74.0 15.7 %all_to_all.33.recv_ref = f32[32,16,128]{2,1,0:T(8,128)S(1)} all-to-all(f32[32,16,128]{2,1,0:T(8,128)S(1)} %get-tuple-element.20), channel_id=1, replica_groups={{320,336,352,368,384,400,416,432,448,464,480,496,0,16,32,48,64,80,96,11..., dimensions={0} | all-to-all | bytes 524288 | tf_op jit(solution)/shard_map/all_to_all | solution.py:277
  89.7 1.2 %shard_map.85 = f32[32,48]{1,0:T(8,128)} custom-call(f32[32,16,128]{2,1,0:T(8,128)S(1)} %all_to_all.33.recv_ref, f32[32,48]{1,0:T(8,128)S(1)} %get-tuple-element.21.sigma_ref, f32[32,48]{1,0:T(8,128)S(1)} %copy-done.4, f32[32,32]{1,0:T(8,128)S(1)} %copy-done.7), custom_call_target="tpu_custom_call" | custom-call | tf_op jit(solution)/shard_map/pallas_call | solution.py:198
  (6 shorter events, 0.0 us)
Async XLA Ops:
  0.6 53.3 %copy-start = (f32[1,3,4,256,256]{4,3,2,1,0:T(8,128)S(1)}, f32[1,3,4,256,256]{4,3,2,1,0:T(8,128)}, u32[]{:S(2)}) copy-start(f32[1,3,4,256,256]{4,3,2,1,0:T(8,128)} %param.6) | copy-start | bytes 9437188
  0.6 0.9 copy-start.3
  2.3 23.7 %all-to-all-start = ((f32[16,1,1536]{2,1,0:T(1,128)}), f32[16,1,1536]{2,1,0:T(1,128)S(1)}, u32[]{:S(2)}, u32[]{:S(2)}) async-start(f32[16,1,1536]{2,1,0:T(1,128)} %shard_map.78), calls=%async_computation | async-start | bytes 196608 | tf_op jit(solution)/shard_map/all_to_all | solution.py:227
  19.6 4.6 %collective-permute-start = (f32[6,32,256]{2,1,0:T(8,128)}, f32[6,32,256]{2,1,0:T(8,128)}, u32[]{:S(2)}, u32[]{:S(2)}) collective-permute-start(f32[6,32,256]{2,1,0:T(8,128)} %bitcast.9), channel_id=1, source_target_pairs={{0,16},{16,0},{32,48},{48,32},{64,80},{80,64},{96,112},{112,96},{1... | collective-permute-start | bytes 589832 | tf_op jit(solution)/shard_map/ppermute | solution.py:229
  26.0 11.5 %all-to-all-start.1 = ((s32[16,2,128]{2,1,0:T(2,128)}), s32[16,2,128]{2,1,0:T(2,128)S(1)}, u32[]{:S(2)}, u32[]{:S(2)}) async-start(s32[16,2,128]{2,1,0:T(2,128)} %bitcast.2), calls=%async_computation.1 | async-start | bytes 32768 | tf_op jit(solution)/shard_map/all_to_all | solution.py:242
  35.2 0.6 copy-start.1
  35.9 0.6 copy-start.5
  37.5 16.4 %copy-start.2 = (f32[32,768]{1,0:T(8,128)S(1)}, f32[32,768]{1,0:T(8,128)}, u32[]{:S(2)}) copy-start(f32[32,768]{1,0:T(8,128)} %copy-done.1) | copy-start | bytes 294916
  37.5 16.4 %copy-start.8 = (s32[1,3,4]{2,0,1:T(1,128)S(1)}, s32[1,3,4]{2,0,1:T(1,128)}, u32[]{:S(2)}) copy-start(s32[1,3,4]{2,0,1:T(1,128)} %param.7) | copy-start | bytes 148
  37.6 16.4 %copy-start.9 = (s32[1,192]{1,0:T(1,128)S(1)}, s32[1,192]{1,0:T(1,128)}, u32[]{:S(2)}) copy-start(s32[1,192]{1,0:T(1,128)} %table_ref.1) | copy-start | bytes 2308
  37.8 35.3 %copy-start.6 = (f32[32,32]{1,0:T(8,128)S(1)}, f32[32,32]{1,0:T(8,128)}, u32[]{:S(2)}) copy-start(f32[32,32]{1,0:T(8,128)} %copy-done.5) | copy-start | bytes 12292
  54.0 35.7 %copy-start.4 = (f32[32,48]{1,0:T(8,128)S(1)}, f32[32,48]{1,0:T(8,128)}, u32[]{:S(2)}) copy-start(f32[32,48]{1,0:T(8,128)} %basis_ref.3) | copy-start | bytes 18436
  54.0 35.7 %copy-start.7 = (f32[32,32]{1,0:T(8,128)S(1)}, f32[32,32]{1,0:T(8,128)}, u32[]{:S(2)}) copy-start(f32[32,32]{1,0:T(8,128)} %ritz_ref.1) | copy-start | bytes 12292

commit v6 on v5

--- a/solution.py
+++ b/solution.py
@@ -107,7 +107,17 @@
     return top, rest
 
 
-def basis_kernel(packed_ref, out_ref, rows):
+def fold(value):
+    quarter = value.shape[0] // 4
+    return jnp.concatenate([value[i * quarter : (i + 1) * quarter] for i in range(4)], axis=1)
+
+
+def unfold(rows):
+    width = rows.shape[1] // 4
+    return jnp.concatenate([rows[:, i * width : (i + 1) * width] for i in range(4)], axis=0)
+
+
+def basis_kernel(packed_ref, out_ref, gram_ref, rows):
     groups = packed_ref.shape[0]
     chunk = out_ref.shape[1] // groups
     for group in range(groups):
@@ -115,11 +125,10 @@
         for row in range(PACKED):
             rows[row : row + 1] = packed_ref[place, :, row * LANES : (row + 1) * LANES]
         out_ref[:, group * chunk : (group + 1) * chunk] = unpack(rows[:PACKED], chunk)
-
-
-def gram_kernel(basis_ref, out_ref):
-    basis = basis_ref[...]
-    out_ref[...] = lax.dot_general(basis, basis, NT, precision=HIGH, preferred_element_type=jnp.float32)
+    basis = out_ref[...]
+    gram_ref[...] = fold(
+        lax.dot_general(basis, basis, NT, precision=HIGH, preferred_element_type=jnp.float32)
+    )
 
 
 def partial_kernel(stored, cols_ref, table_ref, blocks_ref, chosen_ref, basis_ref, out_ref, part):
@@ -150,9 +159,9 @@
         put_rows(out_ref, place, PACKED, tail)
 
 
-def sum_kernel(recv_ref, gram_ref, sigma_ref, keep_ref, out_ref, rows):
+def sum_kernel(recv_ref, gram_ref, sigma_ref, out_ref, rows):
     vectors, chunk = sigma_ref.shape
-    half, quarter = vectors // 2, vectors // 4
+    quarter = vectors // 4
     for row in range(PACKED + quarter):
         here = slice(row * LANES, (row + 1) * LANES)
         total = recv_ref[0, :, here]
@@ -160,33 +169,27 @@
             total = total + recv_ref[group, :, here]
         place = row if row < PACKED else row - PACKED + 16
         rows[place : place + 1] = total
-    sigma = unpack(rows[:PACKED], chunk)
-    sigma_ref[...] = sigma
-    keep_ref[...] = sigma
-    tail = rows[16 : 16 + quarter]
-    moments = jnp.concatenate([tail[:, i * vectors : (i + 1) * vectors] for i in range(4)], axis=0)
-    gram = gram_ref[...]
-    packed = jnp.concatenate([moments[:half], moments[half:], gram[:half], gram[half:]], axis=1)
+    packed = jnp.concatenate([rows[16 : 16 + quarter], gram_ref[...]], axis=0)
     for dest in range(out_ref.shape[0]):
         out_ref[dest] = packed
-
-
-def final_kernel(recv_ref, sigma_ref, basis_ref, ritz_ref, out_ref):
+    sigma_ref[...] = unpack(rows[:PACKED], chunk)
+
+
+def final_kernel(recv_ref, kept_ref, basis_ref, ritz_ref, sigma_ref, out_ref):
     total = recv_ref[0]
     for source in range(1, recv_ref.shape[0]):
         total = total + recv_ref[source]
-    nb = ritz_ref.shape[0]
-    moments = jnp.concatenate([total[:, :nb], total[:, nb : 2 * nb]], axis=0)
-    gram = jnp.concatenate([total[:, 2 * nb : 3 * nb], total[:, 3 * nb :]], axis=0)
-    ritz = ritz_ref[...]
+    quarter = total.shape[0] // 2
+    moments, gram = unfold(total[:quarter]), unfold(total[quarter:])
+    ritz, basis, sigma = ritz_ref[...], basis_ref[...], kept_ref[...]
     dot = functools.partial(jnp.dot, precision=HIGH, preferred_element_type=jnp.float32)
     turn = functools.partial(
         lax.dot_general, dimension_numbers=TN, precision=HIGH, preferred_element_type=jnp.float32
     )
-    basis = basis_ref[...]
+    sigma_ref[...] = sigma
     first = moments - dot(gram, ritz)
     both = 2.0 * basis - turn(gram, basis)
-    out_ref[...] = (sigma_ref[...] - turn(ritz, basis)) - turn(first, both)
+    out_ref[...] = (sigma - turn(ritz, basis)) - turn(first, both)
 
 
 def shape(*dims, dtype=jnp.float32):
@@ -216,7 +219,7 @@
     stored, vectors, _ = owned.shape
     nb, chunk = basis.shape
     cols = jnp.transpose(block_cols, (1, 0, 2))
-    half, quarter = nb // 2, nb // 4
+    quarter = nb // 4
     in_hbm = functools.partial(pltpu.with_memory_space_constraint, memory_space=pltpu.HBM)
     quarter = nb // 4
     whole_col = [turned(n_col, COL_FIRST)]
@@ -240,14 +243,13 @@
     )
     requests, packed, other = lax.optimization_barrier((requests, packed, other))
     wanted = lax.all_to_all(requests, "row", 0, 0, tiled=True, axis_index_groups=groups)
-    row_basis = call(
+    row_basis, gram = call(
         basis_kernel,
-        shape(nb, n_col * chunk),
+        (shape(nb, n_col * chunk), shape(quarter, LANES)),
         [VMEM],
         (packed,),
         [pltpu.VMEM((16, LANES), jnp.float32)],
     )
-    gram = call(gram_kernel, shape(nb, nb), [VMEM], (row_basis,))
     pair = call(
         pair_kernel,
         shape(CORES, stored, vectors, size),
@@ -267,19 +269,19 @@
         [pltpu.VMEM((vectors, rows * size), jnp.float32)],
     )
     gathered = lax.all_to_all(partial_sums, "col", 0, 0, tiled=True, axis_index_groups=whole_col)
-    sigma, keep, moments = call(
+    kept, moments = call(
         sum_kernel,
-        (shape(vectors, chunk), shape(vectors, chunk), shape(n_row, half, LANES)),
+        (shape(vectors, chunk), shape(n_row, 2 * quarter, LANES)),
         [VMEM, VMEM],
         (gathered, gram),
         [pltpu.VMEM((24, LANES), jnp.float32)],
     )
     all_moments = lax.all_to_all(moments, "row", 0, 0, tiled=True, axis_index_groups=whole_row)
-    corrections = call(
+    sigma, corrections = call(
         final_kernel,
-        shape(vectors, chunk),
+        (shape(vectors, chunk), shape(vectors, chunk)),
         [VMEM, VMEM, VMEM, VMEM],
-        (all_moments, keep, basis, ritz_terms),
+        (all_moments, kept, basis, ritz_terms),
     )
     return sigma, corrections
 

time: 91.4 us -> 90.7 us (level)
    pallas_call x9 -> x8, Pallas kernels: 7.95 us -> 7.28 us  [call(): pl.pallas_call(kernel, out_shape=outs, in_specs=ins, out_specs=VMEM if si...]
where the time goes in v6:
time: 90.7 us; the launch traced here: 90.2 us
  blocking collectives  49 us (54%)
  starting transfers between devices  29.1 us (32%)
  Pallas kernels  7.28 us (8%)
  local copies, waits for them, and re-layouts  2.17 us (2%)
  waiting for transfers between devices  1.83 us (2%)
    all_to_all x1, starting transfers between devices, per_device(): lax.all_to_all(packed, 'col', 0, 0, tiled=True, axis_index_groups=whole_col)  17.3 us
    all_to_all x1, blocking collectives, per_device(): lax.all_to_all(partial_sums, 'col', 0, 0, tiled=True, axis_index_groups=w...  17.2 us
    all_to_all x1, blocking collectives, per_device(): lax.all_to_all(sent, 'row', 0, 0, tiled=True, axis_index_groups=groups)  16.1 us
    all_to_all x1, blocking collectives, per_device(): lax.all_to_all(moments, 'row', 0, 0, tiled=True, axis_index_groups=whole_...  15.7 us
    all_to_all x1, starting transfers between devices, per_device(): lax.all_to_all(requests, 'row', 0, 0, tiled=True, axis_index_groups=groups)  8.69 us
    pallas_call x8, Pallas kernels, call(): pl.pallas_call(kernel, out_shape=outs, in_specs=ins, out_specs=VMEM if si...  7.28 us
    ppermute x1, starting transfers between devices, per_device(): other = lax.ppermute(owned, 'row', [(i, i ^ 1) for i in range(n_row)])  3.13 us
    unnamed x20, local copies, waits for them, and re-layouts  2.17 us
  transfers between devices with their start and end apart: 3, of which 1 were waited for; matrix products, arithmetic and copies ran while one was open for 0% of the time, Pallas kernels for 3%

profile of v6, /device:TPU:1, one launch (start us, length us, event | category | flops | bytes accessed | tf_op | source)
XLA Modules:
  0.0 90.2 jit_solution(9338297434625133426)
XLA Ops:
  0.6 0.0 copy-start
  0.6 0.0 copy-start.3
  0.7 0.9 copy-done.3
  1.5 0.8 shard_map.78
  2.3 17.3 %all-to-all-start = ((f32[16,1,1536]{2,1,0:T(1,128)}), f32[16,1,1536]{2,1,0:T(1,128)S(1)}, u32[]{:S(2)}, u32[]{:S(2)}) async-start(f32[16,1,1536]{2,1,0:T(1,128)} %shard_map.78), calls=%async_computation | async-start | bytes 196608 | tf_op jit(solution)/shard_map/all_to_all | solution.py:230
  19.6 3.1 %collective-permute-start = (f32[6,32,256]{2,1,0:T(8,128)}, f32[6,32,256]{2,1,0:T(8,128)}, u32[]{:S(2)}, u32[]{:S(2)}) collective-permute-start(f32[6,32,256]{2,1,0:T(8,128)} %bitcast.9), channel_id=1, source_target_pairs={{0,16},{16,0},{32,48},{48,32},{64,80},{80,64},{96,112},{112,96},{1... | collective-permute-start | bytes 589832 | tf_op jit(solution)/shard_map/ppermute | solution.py:232
  22.8 1.4 %shard_map.77 = s32[32,128]{1,0:T(8,128)} custom-call(s32[3,1,4]{2,1,0:T(1,128)} %bitcast.7, s32[1,192]{1,0:T(1,128)} %table_ref.1), custom_call_target="tpu_custom_call" | custom-call | tf_op jit(solution)/shard_map/pallas_call | solution.py:201
  24.2 0.0 collective-permute-done.other_hbm
  24.2 1.8 %all-to-all-done.packed_ref = f32[16,1,1536]{2,1,0:T(1,128)S(1)} async-done(((f32[16,1,1536]{2,1,0:T(1,128)}), f32[16,1,1536]{2,1,0:T(1,128)S(1)}, u32[]{:S(2)}, u32[]{:S(2)}) %all-to-all-start) | async-done | bytes 98336 | tf_op jit(solution)/shard_map/all_to_all | solution.py:230
  26.0 8.7 %all-to-all-start.1 = ((s32[16,2,128]{2,1,0:T(2,128)}), s32[16,2,128]{2,1,0:T(2,128)S(1)}, u32[]{:S(2)}, u32[]{:S(2)}) async-start(s32[16,2,128]{2,1,0:T(2,128)} %bitcast.2), calls=%async_computation.1 | async-start | bytes 32768 | tf_op jit(solution)/shard_map/all_to_all | solution.py:245
  34.7 0.5 shard_map.81
  35.3 0.7 copy-done.1
  35.9 0.6 copy-done.8
  36.5 1.0 %shard_map.79.pair = f32[2,6,32,256]{3,2,1,0:T(8,128)S(1)} custom-call(f32[6,32,256]{2,1,0:T(8,128)} %bitcast.10, f32[6,32,256]{2,1,0:T(8,128)} %collective-permute-done.other_hbm), custom_call_target="tpu_custom_call" | custom-call | tf_op jit(solution)/shard_map/pallas_call | solution.py:201
  37.6 0.0 all-to-all-done.1
  37.6 0.0 copy-start.2
  37.6 0.0 copy-start.6
  37.6 0.0 copy-start.7
  37.6 0.3 shard_map.80
  37.9 0.0 copy-start.9
  37.9 16.1 %all_to_all.31.chosen_ref = f32[32,32,256]{2,1,0:T(8,128)S(1)} all-to-all(f32[32,32,256]{2,1,0:T(8,128)S(1)} %shard_map.80), channel_id=1, replica_groups={{320,352,384,416,448,480,0,32,64,96,128,160,192,224,256,288},{336,368,4..., dimensions={0} | all-to-all | bytes 2097152 | tf_op jit(solution)/shard_map/all_to_all | solution.py:262
  54.0 0.0 copy-done
  54.0 0.0 copy-done.2
  54.0 0.0 copy-done.6
  54.0 0.0 copy-done.7
  54.0 0.0 copy-start.4
  54.0 0.0 copy-start.5
  54.0 2.0 %shard_map.82 = f32[16,1,2560]{2,1,0:T(1,128)S(1)} custom-call(s32[3,1,4]{2,1,0:T(1,128)S(1)} %bitcast.8, s32[1,192]{1,0:T(1,128)S(1)} %copy-done.7, f32[3,4,256,256]{3,2,1,0:T(8,128)S(1)} %bitcast.5, f32[32,32,256]{2,1,0:T(8,128)S(1)} %all_to_all.31.chosen_ref, f32[32,768]{1,0:T(8,128)S(1)} %copy-done.2), custom_call_target="tpu_custom_call" | custom-call | tf_op jit(solution)/shard_map/pallas_call | solution.py:201
  56.0 17.2 %all_to_all.32.recv_ref = f32[16,1,2560]{2,1,0:T(1,128)S(1)} all-to-all(f32[16,1,2560]{2,1,0:T(1,128)S(1)} %shard_map.82), channel_id=1, replica_groups={{10,11,12,13,14,15,0,1,2,3,4,5,6,7,8,9},{26,27,28,29,30,31,16,17,18,19,..., dimensions={0} | all-to-all | bytes 327680 | tf_op jit(solution)/shard_map/all_to_all | solution.py:271
  73.2 0.2 shard_map.83
  73.4 15.7 %all_to_all.33.recv_ref = f32[32,16,128]{2,1,0:T(8,128)S(1)} all-to-all(f32[32,16,128]{2,1,0:T(8,128)S(1)} %get-tuple-element.22), channel_id=1, replica_groups={{320,336,352,368,384,400,416,432,448,464,480,496,0,16,32,48,64,80,96,11..., dimensions={0} | all-to-all | bytes 524288 | tf_op jit(solution)/shard_map/all_to_all | solution.py:279
  89.1 1.1 %shard_map.84 = (f32[32,48]{1,0:T(8,128)}, f32[32,48]{1,0:T(8,128)}) custom-call(f32[32,16,128]{2,1,0:T(8,128)S(1)} %all_to_all.33.recv_ref, f32[32,48]{1,0:T(8,128)S(1)} %get-tuple-element.23.kept_ref, f32[32,48]{1,0:T(8,128)S(1)} %copy-done.4, f32[32,32]{1,0:T(8,128)S(1)} %copy-done.5), custom_call_target="tpu_custom_call" | custom-call | tf_op jit(solution)/shard_map/pallas_call | solution.py:201
  (5 shorter events, 0.0 us)
Async XLA Ops:
  0.6 53.4 %copy-start = (f32[1,3,4,256,256]{4,3,2,1,0:T(8,128)S(1)}, f32[1,3,4,256,256]{4,3,2,1,0:T(8,128)}, u32[]{:S(2)}) copy-start(f32[1,3,4,256,256]{4,3,2,1,0:T(8,128)} %param.6) | copy-start | bytes 9437188
  0.6 0.9 copy-start.3
  2.3 23.7 %all-to-all-start = ((f32[16,1,1536]{2,1,0:T(1,128)}), f32[16,1,1536]{2,1,0:T(1,128)S(1)}, u32[]{:S(2)}, u32[]{:S(2)}) async-start(f32[16,1,1536]{2,1,0:T(1,128)} %shard_map.78), calls=%async_computation | async-start | bytes 196608 | tf_op jit(solution)/shard_map/all_to_all | solution.py:230
  19.6 4.6 %collective-permute-start = (f32[6,32,256]{2,1,0:T(8,128)}, f32[6,32,256]{2,1,0:T(8,128)}, u32[]{:S(2)}, u32[]{:S(2)}) collective-permute-start(f32[6,32,256]{2,1,0:T(8,128)} %bitcast.9), channel_id=1, source_target_pairs={{0,16},{16,0},{32,48},{48,32},{64,80},{80,64},{96,112},{112,96},{1... | collective-permute-start | bytes 589832 | tf_op jit(solution)/shard_map/ppermute | solution.py:232
  26.0 11.5 %all-to-all-start.1 = ((s32[16,2,128]{2,1,0:T(2,128)}), s32[16,2,128]{2,1,0:T(2,128)S(1)}, u32[]{:S(2)}, u32[]{:S(2)}) async-start(s32[16,2,128]{2,1,0:T(2,128)} %bitcast.2), calls=%async_computation.1 | async-start | bytes 32768 | tf_op jit(solution)/shard_map/all_to_all | solution.py:245
  35.3 0.7 copy-start.1
  35.9 0.6 copy-start.8
  37.6 16.4 %copy-start.2 = (f32[32,768]{1,0:T(8,128)S(1)}, f32[32,768]{1,0:T(8,128)}, u32[]{:S(2)}) copy-start(f32[32,768]{1,0:T(8,128)} %copy-done.1) | copy-start | bytes 294916
  37.6 16.4 %copy-start.6 = (s32[1,3,4]{2,0,1:T(1,128)S(1)}, s32[1,3,4]{2,0,1:T(1,128)}, u32[]{:S(2)}) copy-start(s32[1,3,4]{2,0,1:T(1,128)} %param.7) | copy-start | bytes 148
  37.6 16.4 %copy-start.7 = (s32[1,192]{1,0:T(1,128)S(1)}, s32[1,192]{1,0:T(1,128)}, u32[]{:S(2)}) copy-start(s32[1,192]{1,0:T(1,128)} %table_ref.1) | copy-start | bytes 2308
  37.9 35.3 %copy-start.9 = (f32[8,128]{1,0:T(8,128)S(1)}, f32[8,128]{1,0:T(8,128)}, u32[]{:S(2)}) copy-start(f32[8,128]{1,0:T(8,128)} %copy-done.8) | copy-start | bytes 12292
  54.0 35.1 %copy-start.4 = (f32[32,48]{1,0:T(8,128)S(1)}, f32[32,48]{1,0:T(8,128)}, u32[]{:S(2)}) copy-start(f32[32,48]{1,0:T(8,128)} %basis_ref.3) | copy-start | bytes 18436
  54.0 35.1 %copy-start.5 = (f32[32,32]{1,0:T(8,128)S(1)}, f32[32,32]{1,0:T(8,128)}, u32[]{:S(2)}) copy-start(f32[32,32]{1,0:T(8,128)} %ritz_ref.1) | copy-start | bytes 12292

commit v7 on v6

--- a/solution.py
+++ b/solution.py
@@ -131,17 +131,44 @@
     )
 
 
-def partial_kernel(stored, cols_ref, table_ref, blocks_ref, chosen_ref, basis_ref, out_ref, part):
+def partial_kernel(
+    stored,
+    cols_hbm,
+    table_hbm,
+    blocks_ref,
+    chosen_ref,
+    basis_ref,
+    out_ref,
+    part,
+    cols_ref,
+    table_ref,
+    tops,
+    rests,
+    sems,
+):
     rows, per_row, size, _ = blocks_ref.shape
     vectors = chosen_ref.shape[1]
     groups = out_ref.shape[0]
+    copies = [
+        pltpu.make_async_copy(cols_hbm, cols_ref, sems.at[0]),
+        pltpu.make_async_copy(table_hbm, table_ref, sems.at[1]),
+    ]
+    for copy in copies:
+        copy.start()
+    for entry in range(per_row):
+        tops[entry], rests[entry] = split(blocks_ref[0, entry])
+    for copy in copies:
+        copy.wait()
     for row in range(rows):
         total = jnp.zeros((vectors, size), jnp.float32)
         for entry in range(per_row):
             owner = slot_of(cols_ref, table_ref, row, entry) // stored
             place = (owner + chosen_ref.shape[0] - ROW_FIRST) % chosen_ref.shape[0]
             vec_top, vec_rest = split(chosen_ref[place])
-            mat_top, mat_rest = split(blocks_ref[row, entry])
+            if row == 0:
+                mat_top, mat_rest = tops[entry], rests[entry]
+            else:
+                mat_top, mat_rest = split(blocks_ref[row, entry])
             both = jnp.concatenate([vec_top, vec_rest], axis=0)
             first = lax.dot_general(both, mat_top, NT, preferred_element_type=jnp.float32)
             second = lax.dot_general(vec_top, mat_rest, NT, preferred_element_type=jnp.float32)
@@ -264,9 +291,16 @@
     partial_sums = call(
         functools.partial(partial_kernel, stored),
         shape(n_col, 1, (PACKED + quarter) * LANES),
-        [SMEM, SMEM, VMEM, VMEM, VMEM],
-        (cols, block_slot, local, chosen, row_basis),
-        [pltpu.VMEM((vectors, rows * size), jnp.float32)],
+        [HBM, HBM, VMEM, VMEM, VMEM],
+        (in_hbm(cols), in_hbm(block_slot), local, chosen, row_basis),
+        [
+            pltpu.VMEM((vectors, rows * size), jnp.float32),
+            pltpu.SMEM(cols.shape, jnp.int32),
+            pltpu.SMEM(block_slot.shape, jnp.int32),
+            pltpu.VMEM((per_row, size, size), jnp.bfloat16),
+            pltpu.VMEM((per_row, size, size), jnp.bfloat16),
+            pltpu.SemaphoreType.DMA((2,)),
+        ],
     )
     gathered = lax.all_to_all(partial_sums, "col", 0, 0, tiled=True, axis_index_groups=whole_col)
     kept, moments = call(

time: 90.7 us -> 91 us (level)
    unnamed x20 -> x16, local copies, waits for them, and re-layouts: 2.17 us -> 2.13 us
where the time goes in v7:
time: 91 us; the launch traced here: 90.5 us
  blocking collectives  49.1 us (54%)
  starting transfers between devices  29.1 us (32%)
  Pallas kernels  7.56 us (8%)
  local copies, waits for them, and re-layouts  2.13 us (2%)
  waiting for transfers between devices  1.83 us (2%)
    all_to_all x1, starting transfers between devices, per_device(): lax.all_to_all(packed, 'col', 0, 0, tiled=True, axis_index_groups=whole_col)  17.3 us
    all_to_all x1, blocking collectives, per_device(): lax.all_to_all(partial_sums, 'col', 0, 0, tiled=True, axis_index_groups=w...  17.2 us
    all_to_all x1, blocking collectives, per_device(): lax.all_to_all(sent, 'row', 0, 0, tiled=True, axis_index_groups=groups)  16.1 us
    all_to_all x1, blocking collectives, per_device(): lax.all_to_all(moments, 'row', 0, 0, tiled=True, axis_index_groups=whole_...  15.7 us
    all_to_all x1, starting transfers between devices, per_device(): lax.all_to_all(requests, 'row', 0, 0, tiled=True, axis_index_groups=groups)  8.69 us
    pallas_call x8, Pallas kernels, call(): pl.pallas_call(kernel, out_shape=outs, in_specs=ins, out_specs=VMEM if si...  7.56 us
    ppermute x1, starting transfers between devices, per_device(): other = lax.ppermute(owned, 'row', [(i, i ^ 1) for i in range(n_row)])  3.13 us
    unnamed x16, local copies, waits for them, and re-layouts  2.13 us
  transfers between devices with their start and end apart: 3, of which 1 were waited for; matrix products, arithmetic and copies ran while one was open for 0% of the time, Pallas kernels for 3%

profile of v7, /device:TPU:1, one launch (start us, length us, event | category | flops | bytes accessed | tf_op | source)
XLA Modules:
  0.0 90.5 jit_solution(9111204273268123581)
XLA Ops:
  0.6 0.0 copy-start
  0.6 0.0 copy-start.3
  0.7 0.9 copy-done.3
  1.5 0.8 shard_map.78
  2.3 17.3 %all-to-all-start = ((f32[16,1,1536]{2,1,0:T(1,128)}), f32[16,1,1536]{2,1,0:T(1,128)S(1)}, u32[]{:S(2)}, u32[]{:S(2)}) async-start(f32[16,1,1536]{2,1,0:T(1,128)} %shard_map.78), calls=%async_computation | async-start | bytes 196608 | tf_op jit(solution)/shard_map/all_to_all | solution.py:257
  19.6 3.1 %collective-permute-start = (f32[6,32,256]{2,1,0:T(8,128)}, f32[6,32,256]{2,1,0:T(8,128)}, u32[]{:S(2)}, u32[]{:S(2)}) collective-permute-start(f32[6,32,256]{2,1,0:T(8,128)} %bitcast.7), channel_id=1, source_target_pairs={{0,16},{16,0},{32,48},{48,32},{64,80},{80,64},{96,112},{112,96},{1... | collective-permute-start | bytes 589832 | tf_op jit(solution)/shard_map/ppermute | solution.py:259
  22.8 1.4 %shard_map.77 = s32[32,128]{1,0:T(8,128)} custom-call(s32[3,1,4]{2,1,0:T(1,128)} %bitcast.9, s32[1,192]{1,0:T(1,128)} %table_hbm.3), custom_call_target="tpu_custom_call" | custom-call | tf_op jit(solution)/shard_map/pallas_call | solution.py:228
  24.2 0.0 collective-permute-done.other_hbm
  24.2 1.8 %all-to-all-done.packed_ref = f32[16,1,1536]{2,1,0:T(1,128)S(1)} async-done(((f32[16,1,1536]{2,1,0:T(1,128)}), f32[16,1,1536]{2,1,0:T(1,128)S(1)}, u32[]{:S(2)}, u32[]{:S(2)}) %all-to-all-start) | async-done | bytes 98336 | tf_op jit(solution)/shard_map/all_to_all | solution.py:257
  26.0 8.7 %all-to-all-start.1 = ((s32[16,2,128]{2,1,0:T(2,128)}), s32[16,2,128]{2,1,0:T(2,128)S(1)}, u32[]{:S(2)}, u32[]{:S(2)}) async-start(s32[16,2,128]{2,1,0:T(2,128)} %bitcast.2), calls=%async_computation.1 | async-start | bytes 32768 | tf_op jit(solution)/shard_map/all_to_all | solution.py:272
  34.7 0.5 shard_map.81
  35.2 0.0 copy-start.1
  35.2 0.7 copy-done.1
  35.9 0.0 copy-start.6
  35.9 0.6 copy-done.6
  36.5 1.0 %shard_map.79.pair = f32[2,6,32,256]{3,2,1,0:T(8,128)S(1)} custom-call(f32[6,32,256]{2,1,0:T(8,128)} %bitcast.8, f32[6,32,256]{2,1,0:T(8,128)} %collective-permute-done.other_hbm), custom_call_target="tpu_custom_call" | custom-call | tf_op jit(solution)/shard_map/pallas_call | solution.py:228
  37.5 0.0 all-to-all-done.1
  37.5 0.0 copy-start.2
  37.6 0.3 shard_map.80
  37.8 0.0 copy-start.7
  37.8 16.1 %all_to_all.31.chosen_ref = f32[32,32,256]{2,1,0:T(8,128)S(1)} all-to-all(f32[32,32,256]{2,1,0:T(8,128)S(1)} %shard_map.80), channel_id=1, replica_groups={{320,352,384,416,448,480,0,32,64,96,128,160,192,224,256,288},{336,368,4..., dimensions={0} | all-to-all | bytes 2097152 | tf_op jit(solution)/shard_map/all_to_all | solution.py:289
  53.9 0.0 copy-done
  53.9 0.0 copy-done.2
  53.9 0.0 copy-start.4
  54.0 2.3 %shard_map.82 = f32[16,1,2560]{2,1,0:T(1,128)S(1)} custom-call(s32[3,1,4]{2,1,0:T(1,128)} %bitcast.10, s32[1,192]{1,0:T(1,128)} %table_hbm.3, f32[3,4,256,256]{3,2,1,0:T(8,128)S(1)} %bitcast.5, f32[32,32,256]{2,1,0:T(8,128)S(1)} %all_to_all.31.chosen_ref, f32[32,768]{1,0:T(8,128)S(1)} %copy-done.2), custom_call_target="tpu_custom_call" | custom-call | tf_op jit(solution)/shard_map/pallas_call | solution.py:228
  56.2 17.2 %all_to_all.32.recv_ref = f32[16,1,2560]{2,1,0:T(1,128)S(1)} all-to-all(f32[16,1,2560]{2,1,0:T(1,128)S(1)} %shard_map.82), channel_id=1, replica_groups={{10,11,12,13,14,15,0,1,2,3,4,5,6,7,8,9},{26,27,28,29,30,31,16,17,18,19,..., dimensions={0} | all-to-all | bytes 327680 | tf_op jit(solution)/shard_map/all_to_all | solution.py:305
  73.5 0.0 copy-done.7
  73.5 0.2 shard_map.83
  73.6 15.7 %all_to_all.33.recv_ref = f32[32,16,128]{2,1,0:T(8,128)S(1)} all-to-all(f32[32,16,128]{2,1,0:T(8,128)S(1)} %get-tuple-element.22), channel_id=1, replica_groups={{320,336,352,368,384,400,416,432,448,464,480,496,0,16,32,48,64,80,96,11..., dimensions={0} | all-to-all | bytes 524288 | tf_op jit(solution)/shard_map/all_to_all | solution.py:313
  89.4 0.0 copy-done.4
  89.4 0.0 copy-done.5
  89.4 1.1 %shard_map.84 = (f32[32,48]{1,0:T(8,128)}, f32[32,48]{1,0:T(8,128)}) custom-call(f32[32,16,128]{2,1,0:T(8,128)S(1)} %all_to_all.33.recv_ref, f32[32,48]{1,0:T(8,128)S(1)} %get-tuple-element.23.kept_ref, f32[32,48]{1,0:T(8,128)S(1)} %copy-done.4, f32[32,32]{1,0:T(8,128)S(1)} %copy-done.5), custom_call_target="tpu_custom_call" | custom-call | tf_op jit(solution)/shard_map/pallas_call | solution.py:228
  (1 shorter events, 0.0 us)
Async XLA Ops:
  0.6 53.3 %copy-start = (f32[1,3,4,256,256]{4,3,2,1,0:T(8,128)S(1)}, f32[1,3,4,256,256]{4,3,2,1,0:T(8,128)}, u32[]{:S(2)}) copy-start(f32[1,3,4,256,256]{4,3,2,1,0:T(8,128)} %param.6) | copy-start | bytes 9437188
  0.6 0.9 copy-start.3
  2.3 23.7 %all-to-all-start = ((f32[16,1,1536]{2,1,0:T(1,128)}), f32[16,1,1536]{2,1,0:T(1,128)S(1)}, u32[]{:S(2)}, u32[]{:S(2)}) async-start(f32[16,1,1536]{2,1,0:T(1,128)} %shard_map.78), calls=%async_computation | async-start | bytes 196608 | tf_op jit(solution)/shard_map/all_to_all | solution.py:257
  19.6 4.6 %collective-permute-start = (f32[6,32,256]{2,1,0:T(8,128)}, f32[6,32,256]{2,1,0:T(8,128)}, u32[]{:S(2)}, u32[]{:S(2)}) collective-permute-start(f32[6,32,256]{2,1,0:T(8,128)} %bitcast.7), channel_id=1, source_target_pairs={{0,16},{16,0},{32,48},{48,32},{64,80},{80,64},{96,112},{112,96},{1... | collective-permute-start | bytes 589832 | tf_op jit(solution)/shard_map/ppermute | solution.py:259
  26.0 11.5 %all-to-all-start.1 = ((s32[16,2,128]{2,1,0:T(2,128)}), s32[16,2,128]{2,1,0:T(2,128)S(1)}, u32[]{:S(2)}, u32[]{:S(2)}) async-start(s32[16,2,128]{2,1,0:T(2,128)} %bitcast.2), calls=%async_computation.1 | async-start | bytes 32768 | tf_op jit(solution)/shard_map/all_to_all | solution.py:272
  35.2 0.7 copy-start.1
  35.9 0.6 copy-start.6
  37.5 16.4 %copy-start.2 = (f32[32,768]{1,0:T(8,128)S(1)}, f32[32,768]{1,0:T(8,128)}, u32[]{:S(2)}) copy-start(f32[32,768]{1,0:T(8,128)} %copy-done.1) | copy-start | bytes 294916
  37.8 35.6 %copy-start.7 = (f32[8,128]{1,0:T(8,128)S(1)}, f32[8,128]{1,0:T(8,128)}, u32[]{:S(2)}) copy-start(f32[8,128]{1,0:T(8,128)} %copy-done.6) | copy-start | bytes 12292
  53.9 35.4 %copy-start.4 = (f32[32,48]{1,0:T(8,128)S(1)}, f32[32,48]{1,0:T(8,128)}, u32[]{:S(2)}) copy-start(f32[32,48]{1,0:T(8,128)} %basis_ref.3) | copy-start | bytes 18436
  53.9 35.4 %copy-start.5 = (f32[32,32]{1,0:T(8,128)S(1)}, f32[32,32]{1,0:T(8,128)}, u32[]{:S(2)}) copy-start(f32[32,32]{1,0:T(8,128)} %ritz_ref.1) | copy-start | bytes 12292

commit v8 on v6

--- a/solution.py
+++ b/solution.py
@@ -16,7 +16,7 @@
 TN = (((0,), (0,)), ((), ()))
 CORES = 2
 PACKED = 12
-COL_FIRST = 10
+COL_FIRST = 9
 ROW_FIRST = 20
 
 

time: 90.7 us -> 91 us (level)
  no operation moved by 1% of the time
where the time goes in v8:
time: 91 us; the launch traced here: 90.5 us
  blocking collectives  49 us (54%)
  starting transfers between devices  30 us (33%)
  Pallas kernels  7.28 us (8%)
  local copies, waits for them, and re-layouts  2.17 us (2%)
  waiting for transfers between devices  1.32 us (1%)
    all_to_all x1, starting transfers between devices, per_device(): lax.all_to_all(packed, 'col', 0, 0, tiled=True, axis_index_groups=whole_col)  18.2 us
    all_to_all x1, blocking collectives, per_device(): lax.all_to_all(sent, 'row', 0, 0, tiled=True, axis_index_groups=groups)  16.7 us
    all_to_all x1, blocking collectives, per_device(): lax.all_to_all(partial_sums, 'col', 0, 0, tiled=True, axis_index_groups=w...  16.7 us
    all_to_all x1, blocking collectives, per_device(): lax.all_to_all(moments, 'row', 0, 0, tiled=True, axis_index_groups=whole_...  15.5 us
    all_to_all x1, starting transfers between devices, per_device(): lax.all_to_all(requests, 'row', 0, 0, tiled=True, axis_index_groups=groups)  8.69 us
    pallas_call x8, Pallas kernels, call(): pl.pallas_call(kernel, out_shape=outs, in_specs=ins, out_specs=VMEM if si...  7.28 us
    ppermute x1, starting transfers between devices, per_device(): other = lax.ppermute(owned, 'row', [(i, i ^ 1) for i in range(n_row)])  3.13 us
    unnamed x20, local copies, waits for them, and re-layouts  2.17 us
  transfers between devices with their start and end apart: 3, of which 1 were waited for; matrix products, arithmetic and copies ran while one was open for 0% of the time, Pallas kernels for 3%

profile of v8, /device:TPU:1, one launch (start us, length us, event | category | flops | bytes accessed | tf_op | source)
XLA Modules:
  0.0 90.5 jit_solution(6768670200710269856)
XLA Ops:
  0.6 0.0 copy-start
  0.6 0.0 copy-start.3
  0.7 0.9 copy-done.3
  1.5 0.8 shard_map.78
  2.3 18.2 %all-to-all-start = ((f32[16,1,1536]{2,1,0:T(1,128)}), f32[16,1,1536]{2,1,0:T(1,128)S(1)}, u32[]{:S(2)}, u32[]{:S(2)}) async-start(f32[16,1,1536]{2,1,0:T(1,128)} %shard_map.78), calls=%async_computation | async-start | bytes 196608 | tf_op jit(solution)/shard_map/all_to_all | solution.py:230
  20.5 3.1 %collective-permute-start = (f32[6,32,256]{2,1,0:T(8,128)}, f32[6,32,256]{2,1,0:T(8,128)}, u32[]{:S(2)}, u32[]{:S(2)}) collective-permute-start(f32[6,32,256]{2,1,0:T(8,128)} %bitcast.9), channel_id=1, source_target_pairs={{0,16},{16,0},{32,48},{48,32},{64,80},{80,64},{96,112},{112,96},{1... | collective-permute-start | bytes 589832 | tf_op jit(solution)/shard_map/ppermute | solution.py:232
  23.7 1.4 %shard_map.77 = s32[32,128]{1,0:T(8,128)} custom-call(s32[3,1,4]{2,1,0:T(1,128)} %bitcast.7, s32[1,192]{1,0:T(1,128)} %table_ref.1), custom_call_target="tpu_custom_call" | custom-call | tf_op jit(solution)/shard_map/pallas_call | solution.py:201
  25.1 0.0 collective-permute-done.other_hbm
  25.1 1.3 %all-to-all-done.packed_ref = f32[16,1,1536]{2,1,0:T(1,128)S(1)} async-done(((f32[16,1,1536]{2,1,0:T(1,128)}), f32[16,1,1536]{2,1,0:T(1,128)S(1)}, u32[]{:S(2)}, u32[]{:S(2)}) %all-to-all-start) | async-done | bytes 98336 | tf_op jit(solution)/shard_map/all_to_all | solution.py:230
  26.4 8.7 %all-to-all-start.1 = ((s32[16,2,128]{2,1,0:T(2,128)}), s32[16,2,128]{2,1,0:T(2,128)S(1)}, u32[]{:S(2)}, u32[]{:S(2)}) async-start(s32[16,2,128]{2,1,0:T(2,128)} %bitcast.2), calls=%async_computation.1 | async-start | bytes 32768 | tf_op jit(solution)/shard_map/all_to_all | solution.py:245
  35.1 0.5 shard_map.81
  35.7 0.7 copy-done.1
  36.3 0.6 copy-done.8
  36.9 1.0 %shard_map.79.pair = f32[2,6,32,256]{3,2,1,0:T(8,128)S(1)} custom-call(f32[6,32,256]{2,1,0:T(8,128)} %bitcast.10, f32[6,32,256]{2,1,0:T(8,128)} %collective-permute-done.other_hbm), custom_call_target="tpu_custom_call" | custom-call | tf_op jit(solution)/shard_map/pallas_call | solution.py:201
  38.0 0.0 all-to-all-done.1
  38.0 0.0 copy-start.2
  38.0 0.0 copy-start.6
  38.0 0.0 copy-start.7
  38.0 0.3 shard_map.80
  38.3 0.0 copy-start.9
  38.3 16.7 %all_to_all.31.chosen_ref = f32[32,32,256]{2,1,0:T(8,128)S(1)} all-to-all(f32[32,32,256]{2,1,0:T(8,128)S(1)} %shard_map.80), channel_id=1, replica_groups={{320,352,384,416,448,480,0,32,64,96,128,160,192,224,256,288},{336,368,4..., dimensions={0} | all-to-all | bytes 2097152 | tf_op jit(solution)/shard_map/all_to_all | solution.py:262
  55.0 0.0 copy-done
  55.0 0.0 copy-done.2
  55.0 0.0 copy-done.6
  55.0 0.0 copy-done.7
  55.0 0.0 copy-start.4
  55.0 0.0 copy-start.5
  55.1 2.0 %shard_map.82 = f32[16,1,2560]{2,1,0:T(1,128)S(1)} custom-call(s32[3,1,4]{2,1,0:T(1,128)S(1)} %bitcast.8, s32[1,192]{1,0:T(1,128)S(1)} %copy-done.7, f32[3,4,256,256]{3,2,1,0:T(8,128)S(1)} %bitcast.5, f32[32,32,256]{2,1,0:T(8,128)S(1)} %all_to_all.31.chosen_ref, f32[32,768]{1,0:T(8,128)S(1)} %copy-done.2), custom_call_target="tpu_custom_call" | custom-call | tf_op jit(solution)/shard_map/pallas_call | solution.py:201
  57.0 16.7 %all_to_all.32.recv_ref = f32[16,1,2560]{2,1,0:T(1,128)S(1)} all-to-all(f32[16,1,2560]{2,1,0:T(1,128)S(1)} %shard_map.82), channel_id=1, replica_groups={{9,10,11,12,13,14,15,0,1,2,3,4,5,6,7,8},{25,26,27,28,29,30,31,16,17,18,..., dimensions={0} | all-to-all | bytes 327680 | tf_op jit(solution)/shard_map/all_to_all | solution.py:271
  73.7 0.2 shard_map.83
  73.9 15.5 %all_to_all.33.recv_ref = f32[32,16,128]{2,1,0:T(8,128)S(1)} all-to-all(f32[32,16,128]{2,1,0:T(8,128)S(1)} %get-tuple-element.22), channel_id=1, replica_groups={{320,336,352,368,384,400,416,432,448,464,480,496,0,16,32,48,64,80,96,11..., dimensions={0} | all-to-all | bytes 524288 | tf_op jit(solution)/shard_map/all_to_all | solution.py:279
  89.4 1.1 %shard_map.84 = (f32[32,48]{1,0:T(8,128)}, f32[32,48]{1,0:T(8,128)}) custom-call(f32[32,16,128]{2,1,0:T(8,128)S(1)} %all_to_all.33.recv_ref, f32[32,48]{1,0:T(8,128)S(1)} %get-tuple-element.23.kept_ref, f32[32,48]{1,0:T(8,128)S(1)} %copy-done.4, f32[32,32]{1,0:T(8,128)S(1)} %copy-done.5), custom_call_target="tpu_custom_call" | custom-call | tf_op jit(solution)/shard_map/pallas_call | solution.py:201
  (5 shorter events, 0.0 us)
Async XLA Ops:
  0.6 54.4 %copy-start = (f32[1,3,4,256,256]{4,3,2,1,0:T(8,128)S(1)}, f32[1,3,4,256,256]{4,3,2,1,0:T(8,128)}, u32[]{:S(2)}) copy-start(f32[1,3,4,256,256]{4,3,2,1,0:T(8,128)} %param.6) | copy-start | bytes 9437188
  0.6 0.9 copy-start.3
  2.3 24.1 %all-to-all-start = ((f32[16,1,1536]{2,1,0:T(1,128)}), f32[16,1,1536]{2,1,0:T(1,128)S(1)}, u32[]{:S(2)}, u32[]{:S(2)}) async-start(f32[16,1,1536]{2,1,0:T(1,128)} %shard_map.78), calls=%async_computation | async-start | bytes 196608 | tf_op jit(solution)/shard_map/all_to_all | solution.py:230
  20.5 4.6 %collective-permute-start = (f32[6,32,256]{2,1,0:T(8,128)}, f32[6,32,256]{2,1,0:T(8,128)}, u32[]{:S(2)}, u32[]{:S(2)}) collective-permute-start(f32[6,32,256]{2,1,0:T(8,128)} %bitcast.9), channel_id=1, source_target_pairs={{0,16},{16,0},{32,48},{48,32},{64,80},{80,64},{96,112},{112,96},{1... | collective-permute-start | bytes 589832 | tf_op jit(solution)/shard_map/ppermute | solution.py:232
  26.4 11.5 %all-to-all-start.1 = ((s32[16,2,128]{2,1,0:T(2,128)}), s32[16,2,128]{2,1,0:T(2,128)S(1)}, u32[]{:S(2)}, u32[]{:S(2)}) async-start(s32[16,2,128]{2,1,0:T(2,128)} %bitcast.2), calls=%async_computation.1 | async-start | bytes 32768 | tf_op jit(solution)/shard_map/all_to_all | solution.py:245
  35.7 0.7 copy-start.1
  36.3 0.6 copy-start.8
  38.0 17.0 %copy-start.2 = (f32[32,768]{1,0:T(8,128)S(1)}, f32[32,768]{1,0:T(8,128)}, u32[]{:S(2)}) copy-start(f32[32,768]{1,0:T(8,128)} %copy-done.1) | copy-start | bytes 294916
  38.0 17.0 %copy-start.6 = (s32[1,3,4]{2,0,1:T(1,128)S(1)}, s32[1,3,4]{2,0,1:T(1,128)}, u32[]{:S(2)}) copy-start(s32[1,3,4]{2,0,1:T(1,128)} %param.7) | copy-start | bytes 148
  38.0 17.0 %copy-start.7 = (s32[1,192]{1,0:T(1,128)S(1)}, s32[1,192]{1,0:T(1,128)}, u32[]{:S(2)}) copy-start(s32[1,192]{1,0:T(1,128)} %table_ref.1) | copy-start | bytes 2308
  38.3 35.5 %copy-start.9 = (f32[8,128]{1,0:T(8,128)S(1)}, f32[8,128]{1,0:T(8,128)}, u32[]{:S(2)}) copy-start(f32[8,128]{1,0:T(8,128)} %copy-done.8) | copy-start | bytes 12292
  55.0 34.4 %copy-start.4 = (f32[32,48]{1,0:T(8,128)S(1)}, f32[32,48]{1,0:T(8,128)}, u32[]{:S(2)}) copy-start(f32[32,48]{1,0:T(8,128)} %basis_ref.3) | copy-start | bytes 18436
  55.0 34.4 %copy-start.5 = (f32[32,32]{1,0:T(8,128)S(1)}, f32[32,32]{1,0:T(8,128)}, u32[]{:S(2)}) copy-start(f32[32,32]{1,0:T(8,128)} %ritz_ref.1) | copy-start | bytes 12292
